TPU v7x, 32 devices: a whole 2x2x4 slice. The times are simulated.
32 devices in a mesh: grp: 4 (over y, x), dp: 2 (over core), mp: 4 (over z).
Axes of the slice: x: 2, y: 2, z: 4, core: 2. Of those that a mesh axis runs over, the one named last changes fastest.
Arguments:
- tokens: bfloat16 [4, 2048, 768], P('grp', ('dp', 'mp')), may hold values from -6 to 6
- cotangent: bfloat16 [4, 2048, 768], P('grp', ('dp', 'mp')), may hold values from -6 to 6
- modulation: float32 [4, 8, 9216], P('grp', 'dp'), may hold values from -3 to 3
- clip_frames: int32 [4, 8], P('grp', 'dp'), may hold values from 1 to 64, as said below
- clip_patches: int32 [4, 8], P('grp', 'dp'), may hold values from 1 to 21, as said below
- params: float32 [2, 768, 9216], P(None, 'dp', 'mp')
- first_moment: float32 [4, 2, 768, 9216], P('grp', None, 'dp', 'mp'), may hold values from -5 to 5
- second_moment: float32 [4, 2, 768, 9216], P('grp', None, 'dp', 'mp'), may hold values from 0.02048 to 0.2048
- outer_momentum: float32 [2, 768, 9216], P(None, 'dp', 'mp'), may hold values from -0.21875 to 0.21875
Outputs:
- mixed: bfloat16 [4, 2048, 768], P('grp', ('dp', 'mp'))
- input_grad: float32 [4, 2048, 768], P('grp', ('dp', 'mp'))
- first_moment_new: float32 [4, 2, 768, 9216], P('grp', None, 'dp', 'mp')
- second_moment_new: float32 [4, 2, 768, 9216], P('grp', None, 'dp', 'mp')
- outer_delta: float32 [2, 768, 9216], P(None, 'dp', 'mp')
- outer_momentum_new: float32 [2, 768, 9216], P(None, 'dp', 'mp')
- new_weights: float32 [2, 768, 9216], P(None, 'dp', 'mp')
- new_weights_low: bfloat16 [2, 768, 9216], P(None, 'dp', 'mp')
Inputs may be any that keep to these rules, and one draw needn't show every extreme that they name: `clip_frames`: in each segment exactly one clip has 64 frames, the others at most 8; the clips of a segment fill at most 1024 rows. `clip_patches`: the clip with 64 frames has 4 to 8 patches a frame, the others 21 // 2 to 21.
All inputs are finite; a program needn't handle non-finite values.
Results may differ from a plain program's by a relative error of at most 0.02.
Values may be sent and summed in bfloat16 or wider, within the bound.
A program may use at most 192 MiB of HBM per device.

v0:
```python
from functools import partial

import jax
import jax.numpy as jnp
from jax import lax
from jax.sharding import PartitionSpec as P

D = 768
HEADS = 12
HD = 64
FF = 3072
L = 2
STEP = 5
CAP = 1024
SLOTS = 4


ln_eps = 1e-06
neg_fill = -1e30
beta_one = 0.9
beta_two = 0.999
adam_eps = 1e-08
inner_rate = 0.04
decay_rate = 0.1
outer_rate = 0.7
outer_mu = 0.5


def clip_meta(frames, patches):
    clip_sizes = frames * patches
    clip_ends = jnp.cumsum(clip_sizes)
    clip_starts = clip_ends - clip_sizes
    position = jnp.arange(CAP, dtype=jnp.int32)
    clip_index = jnp.sum((position[:, None] >= clip_ends[None, :]).astype(jnp.int32), axis=1)
    onehot_int = (clip_index[:, None] == jnp.arange(SLOTS, dtype=jnp.int32)[None, :]).astype(
        jnp.int32
    )
    live_mask = clip_index < SLOTS
    clip_begin = jnp.sum(onehot_int * clip_starts[None, :], axis=1)
    frame_width = jnp.maximum(jnp.sum(onehot_int * patches[None, :], axis=1), 1)
    offset_in = position - clip_begin
    frame_index = offset_in // frame_width
    patch_index = offset_in - frame_index * frame_width
    space_id = jnp.where(live_mask, clip_index * CAP + frame_index, -1 - position)
    time_id = jnp.where(live_mask, clip_index * CAP + patch_index, -1 - position)
    return (live_mask, onehot_int.astype(jnp.float32), space_id, time_id)


def normalize(values):
    centered = values - jnp.mean(values, axis=-1, keepdims=True)
    inv_std = lax.rsqrt(jnp.mean(centered * centered, axis=-1, keepdims=True) + ln_eps)
    return (centered * inv_std, inv_std)


def norm_back(grad_normed, normed, inv_std):
    inner = grad_normed - jnp.mean(grad_normed, axis=-1, keepdims=True)
    inner = inner - normed * jnp.mean(grad_normed * normed, axis=-1, keepdims=True)
    return inv_std * inner


def contract_rows(left, right):
    return lax.dot_general(
        left, right, (((0,), (0,)), ((), ())), preferred_element_type=jnp.float32
    )


def contract_cols(left, right):
    return lax.dot_general(
        left, right, (((1,), (1,)), ((), ())), preferred_element_type=jnp.float32
    )


def spread_rows(values):
    return lax.all_gather(values, "mp", axis=0, tiled=True)


def spread_grads(values):
    return lax.all_gather(values, "mp", axis=0, tiled=True)


def collect_branch(whole, weight, own_rows):

    def term(row_start, row_count):
        return contract_cols(whole, weight)

    return lax.psum_scatter(
        term(jnp.int32(0), lax.axis_size("mp") * own_rows), "mp", scatter_dimension=0, tiled=True
    )


def collect_input(whole, weight, own_rows):

    def term(row_start, row_count):
        return contract_cols(whole, weight)

    return lax.psum_scatter(
        term(jnp.int32(0), lax.axis_size("mp") * own_rows), "mp", scatter_dimension=0, tiled=True
    )


def split_weight(weight, heads_dev, ff_dev):
    head_width = heads_dev * HD
    return (
        weight[:, : 3 * head_width],
        weight[:, 3 * head_width : 4 * head_width],
        weight[:, 4 * head_width : 4 * head_width + ff_dev],
        weight[:, 4 * head_width + ff_dev :],
    )


def attend(query, keys, values, group_ids):
    total_rows = query.shape[0]
    block_rows = min(512, total_rows)
    block_count = total_rows // block_rows
    score_scale = HD ** (-0.5)

    def block_step(pieces):
        query_block, id_block = pieces
        scores = (
            jnp.einsum("qhd,khd->hqk", query_block, keys, preferred_element_type=jnp.float32)
            * score_scale
        )
        allowed = (id_block[:, None] == group_ids[None, :])[None]
        scores = jnp.where(allowed, scores, neg_fill)
        row_max = jnp.max(scores, axis=-1, keepdims=True)
        raw_exp = jnp.exp(scores - row_max)
        summed = jnp.sum(raw_exp, axis=-1, keepdims=True)
        probs = (raw_exp / summed).astype(jnp.bfloat16)
        result = jnp.einsum("hqk,khd->qhd", probs, values, preferred_element_type=jnp.float32)
        return (result, (row_max + jnp.log(summed))[..., 0])

    blocked_query = query.reshape(block_count, block_rows, query.shape[1], query.shape[2])
    results, log_sums = lax.map(
        block_step, (blocked_query, group_ids.reshape(block_count, block_rows))
    )
    return (results.reshape(total_rows, query.shape[1], query.shape[2]), log_sums)


def attend_back(query, keys, values, out_grad, log_sums, group_ids):
    total_rows = query.shape[0]
    block_rows = min(512, total_rows)
    block_count = total_rows // block_rows
    score_scale = HD ** (-0.5)

    def block_step(carry, pieces):
        key_acc, value_acc = carry
        query_block, grad_block, log_block, id_block = pieces
        scores = (
            jnp.einsum("qhd,khd->hqk", query_block, keys, preferred_element_type=jnp.float32)
            * score_scale
        )
        allowed = (id_block[:, None] == group_ids[None, :])[None]
        scores = jnp.where(allowed, scores, neg_fill)
        probs = jnp.exp(scores - log_block[..., None])
        value_acc = value_acc + jnp.einsum(
            "hqk,qhd->khd",
            probs.astype(jnp.bfloat16),
            grad_block,
            preferred_element_type=jnp.float32,
        )
        prob_grad = jnp.einsum(
            "qhd,khd->hqk", grad_block, values, preferred_element_type=jnp.float32
        )
        row_delta = jnp.sum(probs * prob_grad, axis=-1, keepdims=True)
        score_grad = (probs * (prob_grad - row_delta)).astype(jnp.bfloat16)
        query_grad = (
            jnp.einsum("hqk,khd->qhd", score_grad, keys, preferred_element_type=jnp.float32)
            * score_scale
        )
        key_acc = (
            key_acc
            + jnp.einsum(
                "hqk,qhd->khd", score_grad, query_block, preferred_element_type=jnp.float32
            )
            * score_scale
        )
        return ((key_acc, value_acc), query_grad)

    heads_dev = query.shape[1]
    blocked_shape = (block_count, block_rows, heads_dev, HD)
    zeros_acc = jnp.zeros((total_rows, heads_dev, HD), jnp.float32)
    (key_grad, value_grad), query_grad = lax.scan(
        block_step,
        (zeros_acc, zeros_acc),
        (
            query.reshape(blocked_shape),
            out_grad.reshape(blocked_shape),
            log_sums,
            group_ids.reshape(block_count, block_rows),
        ),
    )
    return (query_grad.reshape(total_rows, heads_dev, HD), key_grad, value_grad)


def layer_forward(stream, modulate, weight, group_ids, heads_dev, ff_dev, own_rows):
    w_qkv, w_out, w_up, w_down = split_weight(weight, heads_dev, ff_dev)
    head_width = heads_dev * HD
    normed_one, inv_one = normalize(stream)
    lifted_one = (normed_one * (1.0 + modulate[:, 1]) + modulate[:, 0]).astype(jnp.bfloat16)
    whole_one = spread_rows(lifted_one)
    total_rows = whole_one.shape[0]
    qkv = jnp.dot(whole_one, w_qkv, preferred_element_type=jnp.float32).astype(jnp.bfloat16)
    query = qkv[:, :head_width].reshape(total_rows, heads_dev, HD)
    keys = qkv[:, head_width : 2 * head_width].reshape(total_rows, heads_dev, HD)
    values = qkv[:, 2 * head_width :].reshape(total_rows, heads_dev, HD)
    attended, log_sums = attend(query, keys, values, group_ids)
    attended = attended.reshape(total_rows, head_width).astype(jnp.bfloat16)
    branch = collect_branch(attended, w_out, own_rows)
    middle = stream + modulate[:, 2] * branch
    normed_two, inv_two = normalize(middle)
    lifted_two = (normed_two * (1.0 + modulate[:, 4]) + modulate[:, 3]).astype(jnp.bfloat16)
    whole_two = spread_rows(lifted_two)
    hidden = jnp.dot(whole_two, w_up, preferred_element_type=jnp.float32)
    active = jax.nn.gelu(hidden, approximate=False).astype(jnp.bfloat16)
    update = collect_branch(active, w_down, own_rows)
    stored = (
        normed_one,
        inv_one,
        whole_one,
        query,
        keys,
        values,
        attended,
        log_sums,
        normed_two,
        inv_two,
        whole_two,
        hidden,
        active,
    )
    return (middle + modulate[:, 5] * update, stored)


def layer_backward(gradient, stored, modulate, weight, group_ids, heads_dev, ff_dev, own_rows):
    w_qkv, w_out, w_up, w_down = split_weight(weight, heads_dev, ff_dev)
    (
        normed_one,
        inv_one,
        whole_one,
        query,
        keys,
        values,
        attended,
        log_sums,
        normed_two,
        inv_two,
        whole_two,
        hidden,
        active,
    ) = stored
    head_width = heads_dev * HD
    total_rows = whole_one.shape[0]
    down_grad = spread_grads((modulate[:, 5] * gradient).astype(jnp.bfloat16))
    grad_down = contract_rows(down_grad, active)
    active_grad = jnp.dot(down_grad, w_down, preferred_element_type=jnp.float32)
    gelu_fn = partial(jax.nn.gelu, approximate=False)
    gelu_out, gelu_back = jax.vjp(gelu_fn, hidden)
    hidden_grad = gelu_back(active_grad)[0].astype(jnp.bfloat16)
    grad_up = contract_rows(whole_two, hidden_grad)
    lifted_grad_two = collect_input(hidden_grad, w_up, own_rows)
    middle_grad = gradient + norm_back(
        lifted_grad_two * (1.0 + modulate[:, 4]), normed_two, inv_two
    )
    branch_grad = spread_grads((modulate[:, 2] * middle_grad).astype(jnp.bfloat16))
    grad_out = contract_rows(branch_grad, attended)
    attended_grad = jnp.dot(branch_grad, w_out, preferred_element_type=jnp.float32).astype(
        jnp.bfloat16
    )
    attended_grad = attended_grad.reshape(total_rows, heads_dev, HD)
    query_grad, key_grad, value_grad = attend_back(
        query, keys, values, attended_grad, log_sums, group_ids
    )
    qkv_grad = jnp.concatenate(
        [
            query_grad.reshape(total_rows, head_width),
            key_grad.reshape(total_rows, head_width),
            value_grad.reshape(total_rows, head_width),
        ],
        axis=1,
    ).astype(jnp.bfloat16)
    grad_qkv = contract_rows(whole_one, qkv_grad)
    lifted_grad_one = collect_input(qkv_grad, w_qkv, own_rows)
    stream_grad = middle_grad + norm_back(
        lifted_grad_one * (1.0 + modulate[:, 1]), normed_one, inv_one
    )
    return (stream_grad, jnp.concatenate([grad_qkv, grad_out, grad_up, grad_down], axis=1))


def body(
    tokens,
    cotangent,
    modulation,
    clip_frames,
    clip_patches,
    params,
    first_moment,
    second_moment,
    outer_momentum,
):
    own_rows = tokens.shape[1]
    mp_rank = lax.axis_index("mp")
    heads_dev = HEADS // lax.axis_size("mp")
    ff_dev = FF // lax.axis_size("mp")
    live_mask, onehot, space_id, time_id = clip_meta(clip_frames[0], clip_patches[0])
    own_live = lax.dynamic_slice_in_dim(live_mask, mp_rank * own_rows, own_rows, 0)
    own_hot = lax.dynamic_slice_in_dim(onehot, mp_rank * own_rows, own_rows, 0)
    modulate = jnp.dot(
        own_hot, modulation[0], precision=lax.Precision.HIGHEST, preferred_element_type=jnp.float32
    ).reshape(own_rows, L, 6, D)
    weights = lax.all_gather(params.astype(jnp.bfloat16), "dp", axis=1, tiled=True)
    stream = tokens[0].astype(jnp.float32)
    saved = []
    for layer_index in range(L):
        group_ids = space_id if layer_index % 2 == 0 else time_id
        stream, stored = layer_forward(
            stream,
            modulate[:, layer_index],
            weights[layer_index],
            group_ids,
            heads_dev,
            ff_dev,
            own_rows,
        )
        saved.append(stored)
    mixed = stream.astype(jnp.bfloat16)
    gradient = cotangent[0].astype(jnp.float32) * own_live[:, None].astype(jnp.float32)
    layer_grads = [None] * L
    for layer_index in reversed(range(L)):
        group_ids = space_id if layer_index % 2 == 0 else time_id
        gradient, weight_grad = layer_backward(
            gradient,
            saved[layer_index],
            modulate[:, layer_index],
            weights[layer_index],
            group_ids,
            heads_dev,
            ff_dev,
            own_rows,
        )
        layer_grads[layer_index] = weight_grad
    reduced = lax.psum_scatter(
        jnp.stack(layer_grads).astype(jnp.bfloat16), "dp", scatter_dimension=1, tiled=True
    ).astype(jnp.float32)
    moment_one = beta_one * first_moment[0] + (1 - beta_one) * reduced
    moment_two = beta_two * second_moment[0] + (1 - beta_two) * reduced * reduced
    step_size = (
        moment_one / (1 - beta_one**STEP) / (jnp.sqrt(moment_two / (1 - beta_two**STEP)) + adam_eps)
    )
    inner_new = params - inner_rate * (step_size + decay_rate * params)
    difference = params - inner_new
    group_count = lax.axis_size("grp")
    average = lax.psum(difference.astype(jnp.bfloat16), "grp").astype(jnp.float32) / group_count
    momentum = outer_mu * outer_momentum + average
    updated = params - outer_rate * (average + outer_mu * momentum)
    return (
        mixed[None],
        gradient[None],
        moment_one[None],
        moment_two[None],
        average,
        momentum,
        updated,
        updated.astype(jnp.bfloat16),
    )


def solution(mesh):
    in_specs = (
        P("grp", ("dp", "mp"), None),
        P("grp", ("dp", "mp"), None),
        P("grp", "dp", None),
        P("grp", "dp"),
        P("grp", "dp"),
        P(None, "dp", "mp"),
        P("grp", None, "dp", "mp"),
        P("grp", None, "dp", "mp"),
        P(None, "dp", "mp"),
    )
    out_specs = (
        P("grp", ("dp", "mp"), None),
        P("grp", ("dp", "mp"), None),
        P("grp", None, "dp", "mp"),
        P("grp", None, "dp", "mp"),
        P(None, "dp", "mp"),
        P(None, "dp", "mp"),
        P(None, "dp", "mp"),
        P(None, "dp", "mp"),
    )
    return jax.shard_map(body, mesh=mesh, in_specs=in_specs, out_specs=out_specs, check_vma=False)
```

profile of v0, /device:TPU:0, one launch (start us, length us, event | category | flops | bytes accessed | tf_op | source)
XLA Modules:
  0.0 1196.7 jit_solution(3356031956929100414)
XLA Ops:
  39.8 33.9 %all-gather.10.cloned.1.call-done = bf16[1024,768]{1,0:T(8,128)(2,1)} async-done(((bf16[256,768]{1,0:T(8,128)(2,1)}), bf16[1024,768]{1,0:T(8,128)(2,1)}) %all-gather.10.cloned.1.call-update) | async-done | bytes 1572880 | tf_op jit(solution)/shard_map/all_gather | solution.py:74
  77.0 11.6 while.54
  93.5 59.2 %reduce-scatter.12.cloned.1.call-done = f32[256,768]{1,0:T(8,128)} async-done(((f32[1024,768]{1,0:T(8,128)}), f32[256,768]{1,0:T(8,128)}) %reduce-scatter.12.cloned.1.call-update) | async-done | bytes 786448 | tf_op jit(solution)/shard_map/reduce_scatter | solution.py:86
  157.4 36.8 %all-gather.14.cloned.1.call-done = bf16[1024,768]{1,0:T(8,128)(2,1)} async-done(((bf16[256,768]{1,0:T(8,128)(2,1)}), bf16[1024,768]{1,0:T(8,128)(2,1)}) %all-gather.14.cloned.1.call-update) | async-done | bytes 1572880 | tf_op jit(solution)/shard_map/all_gather | solution.py:74
  210.5 59.2 %reduce-scatter.14.cloned.1.call-done = f32[256,768]{1,0:T(8,128)} async-done(((f32[1024,768]{1,0:T(8,128)}), f32[256,768]{1,0:T(8,128)}) %reduce-scatter.14.cloned.1.call-update) | async-done | bytes 786448 | tf_op jit(solution)/shard_map/reduce_scatter | solution.py:86
  274.0 37.2 %all-gather.16.cloned.1.call-done = bf16[1024,768]{1,0:T(8,128)(2,1)} async-done(((bf16[256,768]{1,0:T(8,128)(2,1)}), bf16[1024,768]{1,0:T(8,128)(2,1)}) %all-gather.16.cloned.1.call-update) | async-done | bytes 1572880 | tf_op jit(solution)/shard_map/all_gather | solution.py:74
  314.5 11.6 while.55
  330.6 58.9 %reduce-scatter.16.cloned.1.call-done = f32[256,768]{1,0:T(8,128)} async-done(((f32[1024,768]{1,0:T(8,128)}), f32[256,768]{1,0:T(8,128)}) %reduce-scatter.16.cloned.1.call-update) | async-done | bytes 786448 | tf_op jit(solution)/shard_map/reduce_scatter | solution.py:86
  395.0 36.5 %all-gather.18.cloned.1.call-done = bf16[1024,768]{1,0:T(8,128)(2,1)} async-done(((bf16[256,768]{1,0:T(8,128)(2,1)}), bf16[1024,768]{1,0:T(8,128)(2,1)}) %all-gather.18.cloned.1.call-update) | async-done | bytes 1572880 | tf_op jit(solution)/shard_map/all_gather | solution.py:74
  443.0 26.6 %all-gather.20.cloned.1.call-done = bf16[1024,768]{1,0:T(8,128)(2,1)} async-done(((bf16[256,768]{1,0:T(8,128)(2,1)}), bf16[1024,768]{1,0:T(8,128)(2,1)}) %all-gather.20.cloned.1.call-update) | async-done | bytes 1572880 | tf_op jit(solution)/shard_map/all_gather | solution.py:78
  485.8 54.3 %reduce-scatter.20.cloned.1.call-done = f32[256,768]{1,0:T(8,128)} async-done(((f32[1024,768]{1,0:T(8,128)}), f32[256,768]{1,0:T(8,128)}) %reduce-scatter.20.cloned.1.call-update) | async-done | bytes 786448 | tf_op jit(solution)/shard_map/reduce_scatter | solution.py:96
  541.8 60.9 %reduce-scatter.18.cloned.1.call-done = f32[256,768]{1,0:T(8,128)} async-done(((f32[1024,768]{1,0:T(8,128)}), f32[256,768]{1,0:T(8,128)}) %reduce-scatter.18.cloned.1.call-update) | async-done | bytes 786448 | tf_op jit(solution)/shard_map/reduce_scatter | solution.py:86
  606.7 37.0 %all-gather.22.cloned.1.call-done = bf16[1024,768]{1,0:T(8,128)(2,1)} async-done(((bf16[256,768]{1,0:T(8,128)(2,1)}), bf16[1024,768]{1,0:T(8,128)(2,1)}) %all-gather.22.cloned.1.call-update) | async-done | bytes 1572880 | tf_op jit(solution)/shard_map/all_gather | solution.py:78
  647.1 29.1 %while.56 = (s32[]{:T(128)}, f32[1024,3,64]{0,2,1:T(8,128)}, f32[1024,3,64]{0,2,1:T(8,128)}, bf16[2,512,3,64]{1,3,2,0:T(8,128)(2,1)}, bf16[2,512,3,64]{1,3,2,0:T...) while((s32[]{:T(128)}, f32[1024,3,64]{0,2,1:T(8,128)}, ...), condition=%wide.region_29.30_spmd.clone, body=%wide.region_27.29_spmd.clone.sunk | while | flops 1031830016 | bytes 118906888 | solution.py:182
  684.4 59.2 %reduce-scatter.22.cloned.1.call-done = f32[256,768]{1,0:T(8,128)} async-done(((f32[1024,768]{1,0:T(8,128)}), f32[256,768]{1,0:T(8,128)}) %reduce-scatter.22.cloned.1.call-update) | async-done | bytes 786448 | tf_op jit(solution)/shard_map/reduce_scatter | solution.py:96
  748.5 36.8 %all-gather.24.cloned.1.call-done = bf16[1024,768]{1,0:T(8,128)(2,1)} async-done(((bf16[256,768]{1,0:T(8,128)(2,1)}), bf16[1024,768]{1,0:T(8,128)(2,1)}) %all-gather.24.cloned.1.call-update) | async-done | bytes 1572880 | tf_op jit(solution)/shard_map/all_gather | solution.py:78
  796.6 59.2 %reduce-scatter.24.cloned.1.call-done = f32[256,768]{1,0:T(8,128)} async-done(((f32[1024,768]{1,0:T(8,128)}), f32[256,768]{1,0:T(8,128)}) %reduce-scatter.24.cloned.1.call-update) | async-done | bytes 786448 | tf_op jit(solution)/shard_map/reduce_scatter | solution.py:96
  875.6 22.4 %all-gather.26.cloned.1.call-done = bf16[1024,768]{1,0:T(8,128)(2,1)} async-done(((bf16[256,768]{1,0:T(8,128)(2,1)}), bf16[1024,768]{1,0:T(8,128)(2,1)}) %all-gather.26.cloned.1.call-update) | async-done | bytes 1572880 | tf_op jit(solution)/shard_map/all_gather | solution.py:78
  901.4 32.6 %while.57 = (s32[]{:T(128)}, f32[1024,3,64]{0,2,1:T(8,128)}, f32[1024,3,64]{0,2,1:T(8,128)}, bf16[2,512,3,64]{1,3,2,0:T(8,128)(2,1)}, bf16[2,512,3,64]{1,3,2,0:T...) while((s32[]{:T(128)}, f32[1024,3,64]{0,2,1:T(8,128)}, ...), condition=%wide.region_38.39_spmd.clone, body=%wide.region_36.38_spmd.clone.sunk | while | flops 1031830016 | bytes 114090352 | solution.py:182
  945.7 18.0 %copy.110 = bf16[2,768,2304]{2,0,1:T(2,128)(2,1)} copy(bf16[2,768,2304]{1,2,0:T(8,128)(2,1)} %pad_maximum_fusion) | data formatting | bytes 14155776
  1012.0 16.2 %fusion.84 = (bf16[2,384,2304]{1,2,0:T(8,128)(2,1)}, f32[1,2,384,2304]{2,3,1,0:T(8,128)}, f32[1,2,384,2304]{2,3,1,0:T(8,128)}) fusion(f32[2,384,2304]{1,2,0:T(8,128)} %copy.100, bf16[2,384,2304]{1,2,0:T(8,128)(2,1)} %copy.111, f32[1,2,384,2304]{2,3,1,0:T(8,128)} %copy.96, f32[1,2,384,2304]{2,3,1,0:T(8,128)} %copy.97), kind=kLoop, calls=%fused_computation.105 | loop fusion | flops 31850496 | bytes 42467328 | tf_op jit(solution)/shard_map/convert_element_type | solution.py:352
  1036.4 12.7 %reduce-scatter.26.cloned.1.call-done = f32[256,768]{1,0:T(8,128)} async-done(((f32[1024,768]{1,0:T(8,128)}), f32[256,768]{1,0:T(8,128)}) %reduce-scatter.26.cloned.1.call-update) | async-done | bytes 786448 | tf_op jit(solution)/shard_map/reduce_scatter | solution.py:96
  1069.6 77.5 %all-reduce.2.cloned.1.call-done = bf16[2,384,2304]{1,2,0:T(8,128)(2,1)} async-done(((bf16[2,384,2304]{1,2,0:T(8,128)(2,1)}), bf16[2,384,2304]{1,2,0:T(8,128)(2,1)}) %all-reduce.2.cloned.1.call-update) | async-done | bytes 3538960 | tf_op jit(solution)/shard_map/psum | solution.py:352
  1147.1 12.9 %fusion.183 = (bf16[2,384,2304]{1,2,0:T(8,128)(2,1)}, f32[2,384,2304]{1,2,0:T(8,128)}, f32[2,384,2304]{1,2,0:T(8,128)}, f32[2,384,2304]{1,2,0:T(8,128)}) fusion(f32[2,384,2304]{1,2,0:T(8,128)} %copy.100, f32[2,384,2304]{1,2,0:T(8,128)} %copy.101, bf16[2,384,2304]{1,2,0:T(8,128)(2,1)} %all-reduce.2.cloned.1.call-done), kind=kLoop, calls=%fused_computation.314 | loop fusion | flops 15925248 | bytes 42467328 | tf_op jit(solution)/shard_map/convert_element_type | solution.py:363
  (418 shorter events, 364.7 us)
Async XLA Ops:
  7.2 26.1 %all-gather.12.cloned.1.call-start = ((), (), s32[]{:S(2)}) async-start(), calls=%async_computation.10 | async-start | bytes 10616832 | tf_op jit(solution)/shard_map/all_gather | solution.py:310
  12.4 61.3 %all-gather.10.cloned.1.call-start = ((), (), s32[]{:S(2)}) async-start(), calls=%async_computation.9 | async-start | bytes 1966080 | tf_op jit(solution)/shard_map/all_gather | solution.py:74
  28.3 124.4 %reduce-scatter.12.cloned.1.call-start = ((), (), s32[]{:S(2)}) async-start(), calls=%async_computation.11 | async-start | bytes 3932160 | tf_op jit(solution)/shard_map/reduce_scatter | solution.py:86
  93.5 100.7 %all-gather.14.cloned.1.call-start = ((), (), s32[]{:S(2)}) async-start(), calls=%async_computation.12 | async-start | bytes 1966080 | tf_op jit(solution)/shard_map/all_gather | solution.py:74
  154.3 115.5 %copy-start.16 = (f32[256,768]{1,0:T(8,128)}, f32[256,768]{1,0:T(8,128)S(1)}, u32[]{:S(2)}) copy-start(f32[256,768]{1,0:T(8,128)S(1)} %get-tuple-element.585) | copy-start | bytes 2359300
  156.9 112.8 %reduce-scatter.14.cloned.1.call-start = ((), (), s32[]{:S(2)}) async-start(), calls=%async_computation.13 | async-start | bytes 3932160 | tf_op jit(solution)/shard_map/reduce_scatter | solution.py:86
  210.4 100.8 %all-gather.16.cloned.1.call-start = ((), (), s32[]{:S(2)}) async-start(), calls=%async_computation.14 | async-start | bytes 1966080 | tf_op jit(solution)/shard_map/all_gather | solution.py:74
  271.3 118.3 %copy-start.18 = (f32[256,768]{1,0:T(8,128)}, f32[256,768]{1,0:T(8,128)S(1)}, u32[]{:S(2)}) copy-start(f32[256,768]{1,0:T(8,128)S(1)} %get-tuple-element.577) | copy-start | bytes 2359300
  273.9 115.6 %reduce-scatter.16.cloned.1.call-start = ((), (), s32[]{:S(2)}) async-start(), calls=%async_computation.15 | async-start | bytes 3932160 | tf_op jit(solution)/shard_map/reduce_scatter | solution.py:86
  330.3 61.1 %copy-start.40 = (bf16[1,256,768]{2,1,0:T(8,128)(2,1)S(1)}, bf16[1,256,768]{2,1,0:T(8,128)(2,1)}, u32[]{:S(2)}) copy-start(bf16[1,256,768]{2,1,0:T(8,128)(2,1)} %param.18) | copy-start | bytes 1179652
  330.3 101.1 %all-gather.18.cloned.1.call-start = ((), (), s32[]{:S(2)}) async-start(), calls=%async_computation.16 | async-start | bytes 1966080 | tf_op jit(solution)/shard_map/all_gather | solution.py:74
  394.2 75.5 %all-gather.20.cloned.1.call-start = ((), (), s32[]{:S(2)}) async-start(), calls=%async_computation.18 | async-start | bytes 1966080 | tf_op jit(solution)/shard_map/all_gather | solution.py:78
  394.9 145.2 %reduce-scatter.20.cloned.1.call-start = ((), (), s32[]{:S(2)}) async-start(), calls=%async_computation.19 | async-start | bytes 3932160 | tf_op jit(solution)/shard_map/reduce_scatter | solution.py:96
  480.8 121.9 %reduce-scatter.18.cloned.1.call-start = ((), (), s32[]{:S(2)}) async-start(), calls=%async_computation.17 | async-start | bytes 3932160 | tf_op jit(solution)/shard_map/reduce_scatter | solution.py:86
  485.7 157.9 %all-gather.22.cloned.1.call-start = ((), (), s32[]{:S(2)}) async-start(), calls=%async_computation.20 | async-start | bytes 1966080 | tf_op jit(solution)/shard_map/all_gather | solution.py:78
  606.4 137.2 %reduce-scatter.22.cloned.1.call-start = ((), (), s32[]{:S(2)}) async-start(), calls=%async_computation.21 | async-start | bytes 3932160 | tf_op jit(solution)/shard_map/reduce_scatter | solution.py:96
  684.4 61.0 %copy-start.38 = (f32[256,768]{1,0:T(8,128)S(1)}, f32[256,768]{1,0:T(8,128)}, u32[]{:S(2)}) copy-start(f32[256,768]{1,0:T(8,128)} %get-tuple-element.571) | copy-start | bytes 2359300
  684.4 101.0 %all-gather.24.cloned.1.call-start = ((), (), s32[]{:S(2)}) async-start(), calls=%async_computation.22 | async-start | bytes 1966080 | tf_op jit(solution)/shard_map/all_gather | solution.py:78
  748.1 107.8 %reduce-scatter.24.cloned.1.call-start = ((), (), s32[]{:S(2)}) async-start(), calls=%async_computation.23 | async-start | bytes 3932160 | tf_op jit(solution)/shard_map/reduce_scatter | solution.py:96
  796.5 59.3 %copy-start.57 = (f32[256]{0:T(256)S(1)}, f32[256]{0:T(256)}, u32[]{:S(2)}) copy-start(f32[256]{0:T(256)} %copy-done.56) | copy-start | bytes 3076
  796.6 101.4 %all-gather.26.cloned.1.call-start = ((), (), s32[]{:S(2)}) async-start(), calls=%async_computation.24 | async-start | bytes 1966080 | tf_op jit(solution)/shard_map/all_gather | solution.py:78
  860.6 140.0 %reduce-scatter.28.cloned.1.call-start = ((), (), s32[]{:S(2)}) async-start(), calls=%async_computation.27 | async-start | bytes 10616832
  971.0 78.2 %reduce-scatter.26.cloned.1.call-start = ((), (), s32[]{:S(2)}) async-start(), calls=%async_computation.25 | async-start | bytes 3932160 | tf_op jit(solution)/shard_map/reduce_scatter | solution.py:96
  975.4 171.7 %all-reduce.2.cloned.1.call-start = ((), (), s32[]{:S(2)}) async-start(), calls=%async_computation.26 | async-start | bytes 7077888 | tf_op jit(solution)/shard_map/psum | solution.py:352
  (91 other events, 907.7 us)
Sparse Core Ops, SparseCore 0:
  12.6 20.6 all-gather.11
  35.4 38.2 all-gather.9
  93.6 59.1 reduce-scatter.11
  157.0 37.1 all-gather.13
  210.6 59.1 reduce-scatter.13
  274.1 37.0 all-gather.15
  330.4 59.0 reduce-scatter.15
  394.3 37.1 all-gather.17
  433.6 35.9 all-gather.19
  481.0 59.1 reduce-scatter.19
  542.4 60.2 reduce-scatter.17
  606.5 37.0 all-gather.21
  684.5 59.0 reduce-scatter.21
  748.2 37.1 all-gather.23
  796.7 59.1 reduce-scatter.23
  860.7 37.1 all-gather.25
  971.1 14.3 reduce-scatter.27
  987.8 61.3 reduce-scatter.25
  1053.2 93.8 all-reduce.1
where the time goes:
time: 1210 us; the launch traced here: 1200 us
  waiting for transfers between devices  773 us (64%)
  matrix products  164 us (14%)
  local copies, waits for them, and re-layouts  144 us (12%)
  other arithmetic  96.4 us (8%)
  between operations  15.4 us (1%)
    reduce_scatter x4, waiting for transfers between devices, collect_branch(): lax.psum_scatter(term(jnp.int32(0), lax.axis_size('mp') * own_rows), 'mp'...  238 us
    reduce_scatter x4, waiting for transfers between devices, collect_input(): lax.psum_scatter(term(jnp.int32(0), lax.axis_size('mp') * own_rows), 'mp'...  186 us
    all_gather x4, waiting for transfers between devices, spread_rows(): return lax.all_gather(values, 'mp', axis=0, tiled=True)  144 us
    unnamed x136, local copies, waits for them, and re-layouts  126 us
    all_gather x4, waiting for transfers between devices, spread_grads(): return lax.all_gather(values, 'mp', axis=0, tiled=True)  123 us
    psum x1, waiting for transfers between devices, body(): lax.psum(difference.astype(jnp.bfloat16), 'grp').astype(jnp.float32)  77.5 us
    dot_general x8, matrix products, contract_cols(): lax.dot_general(left, right, (((1,), (1,)), ((), ())), preferred_element_...  34.4 us
  transfers between devices with their start and end apart: 19, of which 18 were waited for; matrix products, arithmetic and copies ran while one was open for 11% of the time, Pallas kernels for 0%

commit v1 on v0

v1 whole, which is shorter than its diff:
```python
from functools import partial

import jax
import jax.numpy as jnp
from jax import lax
from jax.experimental import pallas as pl
from jax.experimental.pallas import tpu as pltpu
from jax.sharding import PartitionSpec as P

D = 768
HEADS = 12
HD = 64
FF = 3072
L = 2
STEP = 5
CAP = 1024
SLOTS = 4
LONGF = 64
ROWS = CAP // 2
CHUNK = 128

ln_eps = 1e-06
neg_fill = -1e30
beta_one = 0.9
beta_two = 0.999
adam_eps = 1e-08
inner_rate = 0.04
decay_rate = 0.1
outer_rate = 0.7
outer_mu = 0.5

f32 = jnp.float32
bf16 = jnp.bfloat16
VM = pltpu.VMEM
SMEM = pltpu.SMEM
MIB = 2**20


def mm(left, right, lc, rc):
    return lax.dot_general(left, right, (((lc,), (rc,)), ((), ())), preferred_element_type=f32)


def moments(values):
    centered = values - jnp.mean(values, axis=-1, keepdims=True)
    inv_std = lax.rsqrt(jnp.mean(centered * centered, axis=-1, keepdims=True) + ln_eps)
    return centered * inv_std, inv_std


def norm_back(grad_normed, normed, inv_std):
    inner = grad_normed - jnp.mean(grad_normed, axis=-1, keepdims=True)
    inner = inner - normed * jnp.mean(grad_normed * normed, axis=-1, keepdims=True)
    return inv_std * inner


def row_mod(clip_col, table):
    total = jnp.where(clip_col == 0, table[0:1, :], 0.0)
    for clip in range(1, SLOTS):
        total = total + jnp.where(clip_col == clip, table[clip : clip + 1, :], 0.0)
    return total


def chunks():
    return [slice(at, at + CHUNK) for at in range(0, ROWS, CHUNK)]


def fetch(w_hbm, buf, sems, layer, low, high):
    copies = []
    for slot in range(4):
        copies.append(
            pltpu.make_async_copy(w_hbm.at[layer, slot, :, low:high], buf.at[slot], sems.at[slot])
        )
        copies[-1].start()
    return copies


def attn_fwd(layer, flag, x, clip, idc, idr, mod, w_hbm, x1, qkv_t, o_t, lse, buf, u_s, acc, sems):
    @pl.when(flag[0] == 1)
    def _():
        width = buf.shape[2]
        heads = 3
        hw = heads * HD
        copies = fetch(w_hbm, buf, sems, layer, 0, width)
        for rows in chunks():
            normed, _ = moments(x[rows, :])
            shift = row_mod(clip[rows, :], mod[0])
            scale = row_mod(clip[rows, :], mod[1])
            u_s[rows, :] = (normed * (1.0 + scale) + shift).astype(bf16)
        acc[...] = jnp.zeros_like(acc)
        for slot in range(4):
            copies[slot].wait()
            part = mm(u_s[...], buf[slot, :, : 3 * hw], 1, 0)
            qkv_t[slot] = part.T.astype(bf16)

            def head_step(head, carry):
                base = pl.multiple_of(head * HD, HD)
                keys = qkv_t[slot, pl.ds(hw + base, HD), :].T
                value_t = qkv_t[slot, pl.ds(2 * hw + base, HD), :]
                for q0 in range(0, ROWS, 256):
                    query_t = qkv_t[slot, pl.ds(base, HD), q0 : q0 + 256]
                    scores = mm(keys, query_t * jnp.asarray(0.125, bf16), 1, 0)
                    allowed = idc[...] == idr[:, q0 : q0 + 256]
                    scores = jnp.where(allowed, scores, neg_fill)
                    top = jnp.max(scores, axis=0, keepdims=True)
                    raw = jnp.exp(scores - top)
                    total = jnp.sum(raw, axis=0, keepdims=True)
                    probs = (raw / total).astype(bf16)
                    o_t[slot, pl.ds(base, HD), q0 : q0 + 256] = mm(value_t, probs, 1, 0).astype(
                        bf16
                    )
                    lse[slot * heads + head, :, q0 : q0 + 256] = top + jnp.log(total)
                return carry

            lax.fori_loop(0, heads, head_step, 0)
            acc[...] += mm(buf[slot, :, 3 * hw :], o_t[slot], 1, 0)
        for rows in chunks():
            gate = row_mod(clip[rows, :], mod[2])
            x1[rows, :] = x[rows, :] + gate * acc[:, rows].T


def mlp_fwd(layer, flag, x, clip, mod, w_hbm, x2, act, dgelu, buf, u_s, acc, sems):
    @pl.when(flag[0] == 1)
    def _():
        half = buf.shape[2] // 2
        attn_width = w_hbm.shape[3] - 2 * half
        copies = fetch(w_hbm, buf, sems, layer, attn_width, w_hbm.shape[3])
        for rows in chunks():
            normed, _ = moments(x[rows, :])
            shift = row_mod(clip[rows, :], mod[3])
            scale = row_mod(clip[rows, :], mod[4])
            u_s[rows, :] = (normed * (1.0 + scale) + shift).astype(bf16)
        acc[...] = jnp.zeros_like(acc)
        for slot in range(4):
            copies[slot].wait()
            for rows in chunks():
                hid = mm(u_s[rows, :], buf[slot, :, :half], 1, 0)
                cdf = 0.5 * (1.0 + lax.erf(hid * 0.7071067811865476))
                pdf = jnp.exp(-0.5 * hid * hid) * 0.3989422804014327
                act[slot, rows, :] = (hid * cdf).astype(bf16)
                dgelu[slot, rows, :] = (cdf + hid * pdf).astype(bf16)
            acc[...] += mm(act[slot], buf[slot, :, half:], 1, 1)
        for rows in chunks():
            gate = row_mod(clip[rows, :], mod[5])
            x2[rows, :] = x[rows, :] + gate * acc[rows, :]


def mlp_bwd(
    layer, flag, g, x, act, dgelu, clip, mod, w_hbm, g1, gw, buf, u_t, d_s, d_t, dh, acc, out, sems, osem
):
    @pl.when(flag[0] == 1)
    def _():
        half = buf.shape[2] // 2
        attn_width = w_hbm.shape[3] - 2 * half
        copies = fetch(w_hbm, buf, sems, layer, attn_width, w_hbm.shape[3])
        for rows in chunks():
            normed, _ = moments(x[rows, :])
            shift = row_mod(clip[rows, :], mod[3])
            scale = row_mod(clip[rows, :], mod[4])
            u_t[:, rows] = (normed * (1.0 + scale) + shift).T.astype(bf16)
            gate = row_mod(clip[rows, :], mod[5])
            down = gate * g[rows, :]
            d_s[rows, :] = down.astype(bf16)
            d_t[:, rows] = down.T.astype(bf16)
        acc[...] = jnp.zeros_like(acc)
        sends = []
        for slot in range(4):
            copies[slot].wait()
            if slot >= 2:
                sends[slot - 2].wait()
            place = slot % 2
            for rows in chunks():
                dact = mm(d_s[rows, :], buf[slot, :, half:], 1, 0)
                dh[rows, :] = (dact * dgelu[slot, rows, :].astype(f32)).astype(bf16)
            out[place, :, :half] = mm(u_t[...], dh[...], 1, 0).astype(bf16)
            out[place, :, half:] = mm(d_t[...], act[slot], 1, 0).astype(bf16)
            sends.append(pltpu.make_async_copy(out.at[place], gw.at[slot], osem.at[place]))
            sends[-1].start()
            acc[...] += mm(dh[...], buf[slot, :, :half], 1, 1)
        for rows in chunks():
            normed, inv_std = moments(x[rows, :])
            scale = row_mod(clip[rows, :], mod[4])
            g1[rows, :] = g[rows, :] + norm_back(acc[rows, :] * (1.0 + scale), normed, inv_std)
        sends[2].wait()
        sends[3].wait()


def attn_bwd(
    layer, flag, g1, x, qkv_t, o_t, lse, clip, idc, idr, mod, w_hbm, g0, gw,
    buf, u_t, d_t, dq, do_s, acc, out, sems, osem
):
    @pl.when(flag[0] == 1)
    def _():
        width = buf.shape[2]
        heads = 3
        hw = heads * HD
        copies = fetch(w_hbm, buf, sems, layer, 0, width)
        for rows in chunks():
            normed, _ = moments(x[rows, :])
            shift = row_mod(clip[rows, :], mod[0])
            scale = row_mod(clip[rows, :], mod[1])
            u_t[:, rows] = (normed * (1.0 + scale) + shift).T.astype(bf16)
            gate = row_mod(clip[rows, :], mod[2])
            d_t[:, rows] = (gate * g1[rows, :]).T.astype(bf16)
        acc[...] = jnp.zeros_like(acc)
        sends = []
        for slot in range(4):
            copies[slot].wait()
            if slot >= 2:
                sends[slot - 2].wait()
            place = slot % 2
            out[place, :, 3 * hw :] = mm(d_t[...], o_t[slot], 1, 1).astype(bf16)
            do_s[...] = mm(buf[slot, :, 3 * hw :], d_t[...], 0, 0).astype(bf16)

            def head_step(head, carry):
                base = pl.multiple_of(head * HD, HD)
                keys_t = qkv_t[slot, pl.ds(hw + base, HD), :]
                keys = keys_t.T
                values = qkv_t[slot, pl.ds(2 * hw + base, HD), :].T
                dk = jnp.zeros((HD, ROWS), f32)
                dv = jnp.zeros((HD, ROWS), f32)
                for q0 in range(0, ROWS, 256):
                    query_t = qkv_t[slot, pl.ds(base, HD), q0 : q0 + 256]
                    grad_t = do_s[pl.ds(base, HD), q0 : q0 + 256]
                    scores = mm(keys, query_t * jnp.asarray(0.125, bf16), 1, 0)
                    allowed = idc[...] == idr[:, q0 : q0 + 256]
                    probs = jnp.where(
                        allowed, jnp.exp(scores - lse[slot * heads + head, :, q0 : q0 + 256]), 0.0
                    )
                    dv = dv + mm(grad_t, probs.astype(bf16), 1, 1)
                    dp = mm(values, grad_t, 1, 0)
                    weighted = probs * dp
                    delta = jnp.sum(weighted, axis=0, keepdims=True)
                    ds = (weighted - probs * delta).astype(bf16)
                    dq[pl.ds(base, HD), q0 : q0 + 256] = (mm(keys_t, ds, 1, 0) * 0.125).astype(bf16)
                    dk = dk + mm(query_t, ds, 1, 1)
                dq[pl.ds(hw + base, HD), :] = (dk * 0.125).astype(bf16)
                dq[pl.ds(2 * hw + base, HD), :] = dv.astype(bf16)
                return carry

            lax.fori_loop(0, heads, head_step, 0)
            out[place, :, : 3 * hw] = mm(u_t[...], dq[...], 1, 1).astype(bf16)
            sends.append(pltpu.make_async_copy(out.at[place], gw.at[slot], osem.at[place]))
            sends[-1].start()
            acc[...] += mm(buf[slot, :, : 3 * hw], dq[...], 1, 0)
        for rows in chunks():
            normed, inv_std = moments(x[rows, :])
            scale = row_mod(clip[rows, :], mod[1])
            g0[rows, :] = g1[rows, :] + norm_back(acc[:, rows].T * (1.0 + scale), normed, inv_std)
        sends[2].wait()
        sends[3].wait()


def any_spec():
    return pl.BlockSpec(memory_space=pl.ANY)


def vm_spec():
    return pl.BlockSpec(memory_space=VM)


def smem_spec():
    return pl.BlockSpec(memory_space=SMEM)


def local_call(kernel, ins, outs, out_spaces, scratch, flops, moved):
    spaces = [smem_spec()] + [
        any_spec() if getattr(a, "ndim", 0) == 4 and a.shape[0] == L and a.shape[1] == 4 else vm_spec()
        for a in ins[1:]
    ]
    return pl.pallas_call(
        kernel,
        out_shape=outs,
        in_specs=spaces,
        out_specs=out_spaces,
        scratch_shapes=scratch,
        compiler_params=pltpu.CompilerParams(vmem_limit_bytes=58 * MIB),
        cost_estimate=pl.CostEstimate(flops=flops, bytes_accessed=moved, transcendentals=0),
    )(*ins)


def run_attn_fwd(layer, flag, x, clip, idc, idr, mod, w):
    sds = jax.ShapeDtypeStruct
    return local_call(
        partial(attn_fwd, layer),
        (flag, x, clip, idc, idr, mod, w),
        (
            sds((ROWS, D), f32),
            sds((4, 9 * HD, ROWS), bf16),
            sds((4, 3 * HD, ROWS), bf16),
            sds((HEADS, 1, ROWS), f32),
        ),
        (vm_spec(),) * 4,
        [
            VM((4, D, 12 * HD), bf16),
            VM((ROWS, D), bf16),
            VM((D, ROWS), f32),
            pltpu.SemaphoreType.DMA((4,)),
        ],
        int(8e9), int(1e7),
    )


def run_mlp_fwd(layer, flag, x, clip, mod, w):
    sds = jax.ShapeDtypeStruct
    unit = FF // 4
    return local_call(
        partial(mlp_fwd, layer),
        (flag, x, clip, mod, w),
        (sds((ROWS, D), f32), sds((4, ROWS, unit), bf16), sds((4, ROWS, unit), bf16)),
        (vm_spec(),) * 3,
        [
            VM((4, D, 2 * unit), bf16),
            VM((ROWS, D), bf16),
            VM((ROWS, D), f32),
            pltpu.SemaphoreType.DMA((4,)),
        ],
        int(8e9), int(1e7),
    )


def run_mlp_bwd(layer, flag, g, x, act, dgelu, clip, mod, w):
    sds = jax.ShapeDtypeStruct
    unit = FF // 4
    return local_call(
        partial(mlp_bwd, layer),
        (flag, g, x, act, dgelu, clip, mod, w),
        (sds((ROWS, D), f32), sds((4, D, 2 * unit), bf16)),
        (vm_spec(), any_spec()),
        [
            VM((4, D, 2 * unit), bf16),
            VM((D, ROWS), bf16),
            VM((ROWS, D), bf16),
            VM((D, ROWS), bf16),
            VM((ROWS, unit), bf16),
            VM((ROWS, D), f32),
            VM((2, D, 2 * unit), bf16),
            pltpu.SemaphoreType.DMA((4,)),
            pltpu.SemaphoreType.DMA((2,)),
        ],
        int(16e9), int(2e7),
    )


def run_attn_bwd(layer, flag, g1, x, qkv_t, o_t, lse, clip, idc, idr, mod, w):
    sds = jax.ShapeDtypeStruct
    return local_call(
        partial(attn_bwd, layer),
        (flag, g1, x, qkv_t, o_t, lse, clip, idc, idr, mod, w),
        (sds((ROWS, D), f32), sds((4, D, 12 * HD), bf16)),
        (vm_spec(), any_spec()),
        [
            VM((4, D, 12 * HD), bf16),
            VM((D, ROWS), bf16),
            VM((D, ROWS), bf16),
            VM((9 * HD, ROWS), bf16),
            VM((3 * HD, ROWS), bf16),
            VM((D, ROWS), f32),
            VM((2, D, 12 * HD), bf16),
            pltpu.SemaphoreType.DMA((4,)),
            pltpu.SemaphoreType.DMA((2,)),
        ],
        int(16e9), int(2e7),
    )


def slot_meta(frames, patches, long_core):
    frames = frames.astype(jnp.int32)
    patches = patches.astype(jnp.int32)
    sizes = frames * patches
    order = jnp.arange(SLOTS, dtype=jnp.int32)
    ends = jnp.sum(jnp.where(order[None, :] <= order[:, None], sizes[None, :], 0), axis=1)
    starts = ends - sizes
    long_hot = frames == LONGF
    long_start = jnp.sum(jnp.where(long_hot, starts, 0))
    long_size = jnp.sum(jnp.where(long_hot, sizes, 0))
    index = jnp.arange(ROWS, dtype=jnp.int32)
    short_pos = jnp.where(index < long_start, index, index + long_size)
    pos = jnp.where(long_core, index + long_start, short_pos)
    clip = jnp.sum((pos[:, None] >= ends[None, :]).astype(jnp.int32), axis=1)
    live = jnp.where(long_core, index < long_size, clip < SLOTS)
    clip = jnp.where(live, clip, SLOTS)
    hot = (clip[:, None] == order[None, :]).astype(jnp.int32)
    begin = jnp.sum(hot * starts[None, :], axis=1)
    width = jnp.maximum(jnp.sum(hot * patches[None, :], axis=1), 1)
    offset = pos - begin
    frame = offset // width
    patch = offset - frame * width
    space_id = jnp.where(live, clip * CAP + frame, -1 - index)
    time_id = jnp.where(live, clip * CAP + patch, -1 - index)
    return pos, live, clip, space_id, time_id


MESH_ID = pl.DeviceIdType.MESH
PIECE = 768
DMA = pltpu.SemaphoreType.DMA


def flip(index, bit):
    return index + bit - 2 * bit * lax.rem(index // bit, 2)


def gather_kernel(
    n_dp, tok, cot, meta, wb, tok_o, cot_o, meta_o, w_o,
    zs, zr, gs, gr, ds, dr, own_l, own_s, own_r, ts, tr, tl, cs, cr, ms, mr, ml,
):
    grp, dp, mp = lax.axis_index("grp"), lax.axis_index("dp"), lax.axis_index("mp")
    rows = wb.shape[1]
    cols = wb.shape[2]
    quarter = tok.shape[0]
    side = PIECE // 2
    pieces = [(layer, at) for layer in range(L) for at in range(0, cols, PIECE)]
    star = 1 + lax.rem(dp, 2)
    is_mid = jnp.logical_or(mp == 1, mp == 2)
    is_main = mp == star
    is_second = jnp.logical_and(is_mid, mp != star)
    other_mid = 3 - mp
    near = jnp.where(mp == 0, 1, 2)
    far = 3 - near
    my_rows = pl.ds(pl.multiple_of(dp * rows, rows), rows)

    def at_mp(where):
        return (grp, dp, where)

    def at_grp(bit):
        return (flip(grp, bit), dp, mp)

    def at_dp(step):
        return (grp, lax.rem(dp + step, n_dp), mp)

    mate = (grp, flip(dp, 1), mp)

    def greet(devices):
        for device in devices:
            pl.semaphore_signal(barrier, inc=1, device_id=device, device_id_type=MESH_ID)
        pl.semaphore_wait(barrier, len(devices))

    barrier = pltpu.get_barrier_semaphore()

    @pl.when(is_mid)
    def _():
        greet(
            [at_mp(0), at_mp(3), at_mp(other_mid), at_grp(1), at_grp(2)]
            + [at_dp(step) for step in range(1, n_dp)]
        )

    @pl.when(jnp.logical_not(is_mid))
    def _():
        greet([at_mp(1), at_mp(2)])

    def remote(src, dst, send, recv, device):
        return pltpu.make_async_remote_copy(
            src_ref=src, dst_ref=dst, send_sem=send, recv_sem=recv,
            device_id=device, device_id_type=MESH_ID,
        )

    def bit_of(k, slot):
        return 1 + (k + slot) % 2

    def half_cols(k, bit, mine):
        index = lax.rem(grp // bit, 2)
        if not mine:
            index = 1 - index
        return pl.ds(pl.multiple_of(pieces[k][1] + index * side, 128), side)

    def z_copy(k, slot, device):
        layer = pieces[k][0]
        span = half_cols(k, bit_of(k, slot), True)
        return remote(
            wb.at[layer, :, span], w_o.at[layer, slot, my_rows, span],
            zs.at[k, slot - 1], zr.at[k, slot - 1], device,
        )

    def g_copy(k, slot):
        layer = pieces[k][0]
        bit = bit_of(k, slot)
        span = half_cols(k, bit, True)
        place = w_o.at[layer, slot, my_rows, span]
        return remote(place, place, gs.at[k, slot - 1], gr.at[k, slot - 1], at_grp(bit))

    def d_copies(k, slot, mine):
        layer = pieces[k][0]
        span = half_cols(k, bit_of(k, slot), mine)
        place = w_o.at[layer, slot, my_rows, span]
        turn = 0 if mine else 1
        return [
            remote(
                place, place, ds.at[k, slot - 1, turn, step - 1], dr.at[k, slot - 1, turn, step - 1],
                at_dp(step),
            )
            for step in range(1, n_dp)
        ]

    def d_arrivals(k, slot, mine):
        layer = pieces[k][0]
        span = half_cols(k, bit_of(k, slot), mine)
        turn = 0 if mine else 1
        result = []
        for step in range(1, n_dp):
            source = lax.rem(dp + n_dp - step, n_dp)
            place = w_o.at[layer, slot, pl.ds(pl.multiple_of(source * rows, rows), rows), span]
            result.append(
                remote(
                    place, place, ds.at[k, slot - 1, turn, step - 1],
                    dr.at[k, slot - 1, turn, step - 1], at_dp(step),
                )
            )
        return result

    def part(ref, index):
        return ref.at[pl.ds(pl.multiple_of(index * quarter, quarter), quarter)]

    def route(src, out, send, recv):
        return remote(src, part(out, mp), send.at[0], recv.at[mp], at_mp(star))

    def pass_on(out, send, recv, index):
        return remote(
            part(out, index), part(out, index), send.at[1 + index], recv.at[4 + index], mate
        )

    both = ((tok, tok_o, ts, tr), (cot, cot_o, cs, cr))

    @pl.when(jnp.logical_not(is_main))
    def _():
        route(tok, tok_o, ts, tr).start()

    @pl.when(is_main)
    def _():
        pltpu.make_async_copy(meta, meta_o, ml.at[0]).start()
        remote(meta, meta_o, ms.at[0], mr.at[0], mate).start()
        for i, (src, out, send, recv) in enumerate(both):
            pltpu.make_async_copy(src, part(out, mp), tl.at[i]).start()

    count = len(pieces)

    @pl.when(jnp.logical_not(is_mid))
    def _():
        for k in range(count):
            if k == 2:
                route(cot, cot_o, cs, cr).start()
            if k >= 2:
                z_copy(k - 2, 1, at_mp(near)).wait_send()
                z_copy(k - 2, 3, at_mp(far)).wait_send()
            z_copy(k, 1, at_mp(near)).start()
            z_copy(k, 3, at_mp(far)).start()
        for k in range(count - 2, count):
            z_copy(k, 1, at_mp(near)).wait_send()
            z_copy(k, 3, at_mp(far)).wait_send()
        route(tok, tok_o, ts, tr).wait_send()
        route(cot, cot_o, cs, cr).wait_send()

    def arrival(out, recv, index):
        return remote(part(out, index), part(out, index), ts.at[0], recv.at[index], mate)

    def second_arrival(out, recv, index):
        return remote(part(out, index), part(out, index), ts.at[0], recv.at[4 + index], mate)

    def spread(which):
        src, out, send, recv = both[which]

        @pl.when(is_main)
        def _():
            pltpu.make_async_copy(src, part(out, mp), tl.at[which]).wait()
            pass_on(out, send, recv, mp).start()
            for index in (other_mid, 0, 3):
                arrival(out, recv, index).wait_recv()
                pass_on(out, send, recv, index).start()

    @pl.when(is_mid)
    def _():
        own = [
            pltpu.make_async_copy(wb.at[layer], w_o.at[layer, 0, my_rows], own_l.at[layer])
            for layer in range(L)
        ]
        shares = [
            [
                remote(
                    wb.at[layer], w_o.at[layer, 0, my_rows],
                    own_s.at[layer, step - 1], own_r.at[layer, step - 1], at_dp(step),
                )
                for step in range(1, n_dp)
            ]
            for layer in range(L)
        ]
        own[0].start()
        for copy in shares[0]:
            copy.start()
        z_copy(0, 2, at_mp(other_mid)).start()
        z_copy(1, 2, at_mp(other_mid)).start()
        spread(0)
        for k in range(count):
            if k == 2:
                own[1].start()
                for copy in shares[1]:
                    copy.start()
                pl.when(is_second)(lambda: route(cot, cot_o, cs, cr).start())
            if k == 4:
                spread(1)
            for slot in (1, 2, 3):
                z_copy(k, slot, at_mp(other_mid)).wait_recv()
                g_copy(k, slot).start()
                for copy in d_copies(k, slot, True):
                    copy.start()
            if k + 2 < count:
                z_copy(k, 2, at_mp(other_mid)).wait_send()
                z_copy(k + 2, 2, at_mp(other_mid)).start()
            if k >= 1:
                for slot in (1, 2, 3):
                    g_copy(k - 1, slot).wait_recv()
                    for copy in d_copies(k - 1, slot, False):
                        copy.start()
        for slot in (1, 2, 3):
            g_copy(count - 1, slot).wait_recv()
            for copy in d_copies(count - 1, slot, False):
                copy.start()
        for k in range(count - 2, count):
            z_copy(k, 2, at_mp(other_mid)).wait_send()
        for k in range(count):
            for slot in (1, 2, 3):
                g_copy(k, slot).wait_send()
                for mine in (True, False):
                    for copy in d_copies(k, slot, mine):
                        copy.wait_send()
                    for copy in d_arrivals(k, slot, mine):
                        copy.wait_recv()
        for layer in range(L):
            own[layer].wait()
            for step in range(1, n_dp):
                shares[layer][step - 1].wait_send()
                source = lax.rem(dp + n_dp - step, n_dp)
                place = w_o.at[layer, 0, pl.ds(pl.multiple_of(source * rows, rows), rows)]
                remote(
                    place, place, own_s.at[layer, step - 1], own_r.at[layer, step - 1], at_dp(step)
                ).wait_recv()

    @pl.when(is_main)
    def _():
        pltpu.make_async_copy(meta, meta_o, ml.at[0]).wait()
        remote(meta, meta_o, ms.at[0], mr.at[0], mate).wait_send()
        for src, out, send, recv in both:
            for index in range(4):
                pass_on(out, send, recv, index).wait_send()

    @pl.when(is_second)
    def _():
        remote(meta, meta_o, ms.at[0], mr.at[0], mate).wait_recv()
        route(tok, tok_o, ts, tr).wait_send()
        route(cot, cot_o, cs, cr).wait_send()
        for src, out, send, recv in both:
            for index in range(4):
                second_arrival(out, recv, index).wait_recv()


def gather_all(tok, cot, meta, wb):
    sds = jax.ShapeDtypeStruct
    n_dp = lax.axis_size("dp")
    rows, cols = wb.shape[1], wb.shape[2]
    count = L * cols // PIECE
    far = n_dp - 1
    return pl.pallas_call(
        partial(gather_kernel, n_dp),
        out_shape=(
            sds((CAP, D), bf16), sds((CAP, D), bf16), sds(meta.shape, f32),
            sds((L, 4, rows * n_dp, cols), bf16),
        ),
        in_specs=[any_spec()] * 4,
        out_specs=(any_spec(),) * 4,
        scratch_shapes=[
            DMA((count, 3)), DMA((count, 3)), DMA((count, 3)), DMA((count, 3)),
            DMA((count, 3, 2, far)), DMA((count, 3, 2, far)),
            DMA((L,)), DMA((L, far)), DMA((L, far)),
            DMA((5,)), DMA((8,)), DMA((2,)), DMA((5,)), DMA((8,)), DMA((1,)), DMA((1,)), DMA((1,)),
        ],
        compiler_params=pltpu.CompilerParams(collective_id=1, has_side_effects=True),
    )(tok, cot, meta, wb)


def adam_kernel(flag, par, mom, var, own, ga, gb, gc, *rest):
    new_m, new_v, diff = rest[-3:]
    keep = jnp.where(flag[0] == 1, own[...].astype(f32), 0.0)
    grad = keep + ga[...].astype(f32) + gb[...].astype(f32) + gc[...].astype(f32)
    one = beta_one * mom[...] + (1 - beta_one) * grad
    two = beta_two * var[...] + (1 - beta_two) * grad * grad
    step = one / (1 - beta_one**STEP) / (jnp.sqrt(two / (1 - beta_two**STEP)) + adam_eps)
    new_m[...] = one
    new_v[...] = two
    diff[...] = (inner_rate * (step + decay_rate * par[...])).astype(bf16)


def row_block(rows):
    return 96 if rows % 96 == 0 else rows


def adam(flag, layer, first, width, par, mom, var, parts, prev):
    rows, cols = par.shape[1], par.shape[2]
    block = row_block(rows)
    sds = jax.ShapeDtypeStruct
    base = first // PIECE
    full = pl.BlockSpec((None, block, PIECE), lambda i, j: (layer, i, base + j))
    piece = pl.BlockSpec((block, PIECE), lambda i, j: (i, j))
    ins = [flag, par, mom, var, *parts]
    specs = [smem_spec(), full, full, full] + [piece] * 4
    aliases = {}
    if prev is not None:
        aliases = {len(ins): 0, len(ins) + 1: 1}
        ins += list(prev)
        specs += [any_spec(), any_spec()]
    return pl.pallas_call(
        adam_kernel,
        grid=(rows // block, width // PIECE),
        out_shape=(sds(par.shape, f32), sds(par.shape, f32), sds((rows, width), bf16)),
        in_specs=specs,
        out_specs=(full, full, piece),
        input_output_aliases=aliases,
        compiler_params=pltpu.CompilerParams(vmem_limit_bytes=48 * MIB),
        cost_estimate=pl.CostEstimate(
            flops=rows * width * 20, bytes_accessed=rows * width * 30, transcendentals=0
        ),
    )(*ins)


def outer_kernel(count, par, mom, *rest):
    total = rest[0][...].astype(f32)
    for other in rest[1:count]:
        total = total + other[...].astype(f32)
    average = total / count
    out_a, out_m, out_w, out_l = rest[-4:]
    momentum = outer_mu * mom[...] + average
    updated = par[...] - outer_rate * (average + outer_mu * momentum)
    out_a[...] = average
    out_m[...] = momentum
    out_w[...] = updated
    out_l[...] = updated.astype(bf16)


def outer(layer, first, width, par, mom, diffs, prev):
    rows, cols = par.shape[1], par.shape[2]
    block = row_block(rows)
    sds = jax.ShapeDtypeStruct
    base = first // PIECE
    full = pl.BlockSpec((None, block, PIECE), lambda i, j: (layer, i, base + j))
    piece = pl.BlockSpec((block, PIECE), lambda i, j: (i, j))
    ins = [par, mom, *diffs]
    specs = [full, full] + [piece] * len(diffs)
    aliases = {}
    if prev is not None:
        aliases = {len(ins) + i: i for i in range(4)}
        ins += list(prev)
        specs += [any_spec()] * 4
    return pl.pallas_call(
        partial(outer_kernel, len(diffs)),
        grid=(rows // block, width // PIECE),
        out_shape=(sds(par.shape, f32),) * 3 + (sds(par.shape, bf16),),
        in_specs=specs,
        out_specs=(full,) * 4,
        input_output_aliases=aliases,
        compiler_params=pltpu.CompilerParams(vmem_limit_bytes=48 * MIB),
        cost_estimate=pl.CostEstimate(
            flops=rows * width * 20, bytes_accessed=rows * width * 30, transcendentals=0
        ),
    )(*ins)


def send_mp(values, pairs):
    return lax.ppermute(values, "mp", pairs)


def body(
    tokens, cotangent, modulation, clip_frames, clip_patches, params, first_moment, second_moment,
    outer_momentum,
):
    n_dp = lax.axis_size("dp")
    n_grp = lax.axis_size("grp")
    dp, mp = lax.axis_index("dp"), lax.axis_index("mp")
    quarter = tokens.shape[1]
    rows, cols = params.shape[1], params.shape[2]
    star = 1 + lax.rem(dp, 2)
    is_mid = jnp.logical_or(mp == 1, mp == 2)
    flag = is_mid.astype(jnp.int32)[None]

    meta = jnp.concatenate(
        [
            modulation[0],
            clip_frames[0].astype(f32)[:, None],
            clip_patches[0].astype(f32)[:, None],
            jnp.zeros((SLOTS, 126), f32),
        ],
        axis=1,
    )
    tok_all, cot_all, meta_all, w = gather_all(tokens[0], cotangent[0], meta, params.astype(bf16))

    mods = meta_all[:, : modulation.shape[2]].reshape(SLOTS, L, 6, D).transpose(1, 2, 0, 3)
    frames = meta_all[:, modulation.shape[2]]
    patches = meta_all[:, modulation.shape[2] + 1]
    pos, live, clip, space_id, time_id = slot_meta(frames, patches, mp == star)
    pick = (pos[:, None] == jnp.arange(CAP, dtype=jnp.int32)[None, :]) & live[:, None]
    pick = pick.astype(bf16)
    clip = clip[:, None]

    x = jnp.dot(pick, tok_all, preferred_element_type=f32)
    gradient = jnp.dot(pick, cot_all, preferred_element_type=f32)
    ids = (space_id, time_id)
    kept = []
    for layer in range(L):
        idc, idr = ids[layer % 2][:, None], ids[layer % 2][None, :]
        x1, qkv_t, o_t, lse = run_attn_fwd(layer, flag, x, clip, idc, idr, mods[layer], w)
        x2, act, dgelu = run_mlp_fwd(layer, flag, x1, clip, mods[layer], w)
        kept.append((x, x1, qkv_t, o_t, lse, act, dgelu))
        x = x2

    back = [
        [((d, s), (d, o)) for d, s, o in ((d, 1 + d % 2, order(d)) for d in range(n_dp))]
        for order in (
            lambda d: 0 if d % 2 == 0 else 3,
            lambda d: 2 if d % 2 == 0 else 1,
            lambda d: 3 if d % 2 == 0 else 0,
        )
    ]
    quarters = [jnp.where(star == 1, a, b) for a, b in ((0, 3), (2, 1), (3, 0))]
    swap = [(d, d ^ 1) for d in range(n_dp)]

    def send_back(values):
        placed = lax.dot_general(
            pick, values.astype(bf16), (((0,), (0,)), ((), ())), preferred_element_type=f32
        ).astype(bf16)
        placed = jnp.where(is_mid, placed, jnp.zeros_like(placed))
        placed = placed + lax.ppermute(placed, "dp", swap)
        mine = lax.dynamic_slice_in_dim(placed, mp * quarter, quarter, 0)
        result = jnp.where(mp == star, mine, jnp.zeros_like(mine))
        for pairs, index in zip(back, quarters):
            piece = lax.dynamic_slice_in_dim(placed, index * quarter, quarter, 0)
            flat = [(a[0] * 4 + a[1], b[0] * 4 + b[1]) for a, b in pairs]
            result = result + lax.ppermute(piece, ("dp", "mp"), flat)
        return result

    total = jnp.sum(clip_frames[0] * clip_patches[0])
    own_live = (mp * quarter + jnp.arange(quarter, dtype=jnp.int32) < total)[:, None]
    mixed = jnp.where(own_live, send_back(x), tokens[0])

    mom, var = first_moment[0], second_moment[0]
    state, done = None, None

    def finish(layer, first, grads, state, done):
        width = grads.shape[2]
        share = lax.psum_scatter(grads, "dp", scatter_dimension=1, tiled=True)
        parts = (
            share[0],
            send_mp(share[1], [(1, 0), (2, 3)]),
            send_mp(share[2], [(1, 2), (2, 1)]),
            send_mp(share[3], [(1, 3), (2, 0)]),
        )
        new_m, new_v, diff = adam(flag, layer, first, width, params, mom, var, parts, state)
        diffs = [diff] + [
            lax.ppermute(diff, "grp", [(g, (g + step) % n_grp) for g in range(n_grp)])
            if n_grp != 4
            else lax.ppermute(diff, "grp", [(g, g ^ step) for g in range(n_grp)])
            for step in range(1, n_grp)
        ]
        done = outer(layer, first, width, params, outer_momentum, diffs, done)
        return (new_m, new_v), done

    for layer in reversed(range(L)):
        idc, idr = ids[layer % 2][:, None], ids[layer % 2][None, :]
        x0, x1, qkv_t, o_t, lse, act, dgelu = kept[layer]
        g1, g_mlp = run_mlp_bwd(layer, flag, gradient, x1, act, dgelu, clip, mods[layer], w)
        state, done = finish(layer, PIECE, g_mlp, state, done)
        gradient, g_attn = run_attn_bwd(
            layer, flag, g1, x0, qkv_t, o_t, lse, clip, idc, idr, mods[layer], w
        )
        state, done = finish(layer, 0, g_attn, state, done)
    input_grad = send_back(gradient).astype(f32)
    average, momentum, updated, low = done
    return (
        mixed[None], input_grad[None], state[0][None], state[1][None], average, momentum, updated, low,
    )


def solution(mesh):
    in_specs = (
        P("grp", ("dp", "mp"), None),
        P("grp", ("dp", "mp"), None),
        P("grp", "dp", None),
        P("grp", "dp"),
        P("grp", "dp"),
        P(None, "dp", "mp"),
        P("grp", None, "dp", "mp"),
        P("grp", None, "dp", "mp"),
        P(None, "dp", "mp"),
    )
    out_specs = (
        P("grp", ("dp", "mp"), None),
        P("grp", ("dp", "mp"), None),
        P("grp", None, "dp", "mp"),
        P("grp", None, "dp", "mp"),
        P(None, "dp", "mp"),
        P(None, "dp", "mp"),
        P(None, "dp", "mp"),
        P(None, "dp", "mp"),
    )
    return jax.shard_map(body, mesh=mesh, in_specs=in_specs, out_specs=out_specs, check_vma=False)
```

time: 1210 us -> 719 us (0.59)
  waiting for transfers between devices: 773 us -> 363 us
  Pallas kernels: 0 us -> 228 us
  matrix products: 164 us -> 9.7 us
  local copies, waits for them, and re-layouts: 144 us -> 30.5 us
  other arithmetic: 96.4 us -> 27.8 us
  starting transfers between devices: 2.19 us -> 37.5 us
    reduce_scatter x8 -> x4, waiting for transfers between devices: 424 us -> 111 us  [finish(): share = lax.psum_scatter(grads, 'dp', scatter_dimension=1, tiled=True)]
    all_gather x9 -> x0, waiting for transfers between devices: 271 us -> none  [the longest x4 144 us: spread_rows(): return lax.all_gather(values, 'mp', axis=0, tiled=True)]
    ppermute x0 -> x32, waiting for transfers between devices: none -> 251 us  [the longest x12 97.3 us: finish(): lax.ppermute(diff, 'grp', [(g, g ^ step) for g in range(n_grp)])]
    pallas_call x0 -> x17, Pallas kernels: none -> 228 us  [the longest x1 98.8 us: gather_all(): pl.pallas_call(partial(gather_kernel, n_dp), out_shape=(sds((CAP, D), bf1...]
    dot_general x53 -> x4, matrix products: 164 us -> 9.7 us  [the longest x1 3.84 us: body(): x = jnp.dot(pick, tok_all, preferred_element_type=f32)]
    unnamed x136 -> x54, local copies, waits for them, and re-layouts: 126 us -> 11.5 us
    psum x1 -> x0, waiting for transfers between devices: 77.5 us -> none  [body(): lax.psum(difference.astype(jnp.bfloat16), 'grp').astype(jnp.float32)]
    convert_element_type x15 -> x2, other arithmetic: 59.5 us -> 6.1 us  [the longest x1 5.18 us: body(): params.astype(bf16)]
  transfers between devices with their start and end apart: 19 -> 36, of which waited for: 18 -> 13; matrix products, arithmetic and copies ran while one was open for 11% -> 4% of each run, Pallas kernels for 0% -> 10%
where the time goes in v1:
time: 719 us; the launch traced here: 711 us
  waiting for transfers between devices  363 us (50%)
  Pallas kernels  228 us (32%)
  starting transfers between devices  37.5 us (5%)
  local copies, waits for them, and re-layouts  30.5 us (4%)
  other arithmetic  27.8 us (4%)
  between operations  14.5 us (2%)
  matrix products  9.7 us (1%)
    reduce_scatter x4, waiting for transfers between devices, finish(): share = lax.psum_scatter(grads, 'dp', scatter_dimension=1, tiled=True)  111 us
    pallas_call x1, Pallas kernels, gather_all(): pl.pallas_call(partial(gather_kernel, n_dp), out_shape=(sds((CAP, D), bf1...  98.8 us
    ppermute x12, waiting for transfers between devices, finish(): lax.ppermute(diff, 'grp', [(g, g ^ step) for g in range(n_grp)])  97.3 us
    ppermute x6, waiting for transfers between devices, send_back(): result = result + lax.ppermute(piece, ('dp', 'mp'), flat)  86.2 us
    pallas_call x8, Pallas kernels, local_call(): pl.pallas_call(kernel, out_shape=outs, in_specs=spaces, out_specs=out_spa...  76.1 us
    ppermute x12, waiting for transfers between devices, send_mp(): return lax.ppermute(values, 'mp', pairs)  65.9 us
    pallas_call x4, Pallas kernels, outer(): pl.pallas_call(partial(outer_kernel, len(diffs)), grid=(rows // block, wi...  26.8 us
    pallas_call x4, Pallas kernels, adam(): pl.pallas_call(adam_kernel, grid=(rows // block, width // PIECE), out_sha...  26.7 us
  transfers between devices with their start and end apart: 36, of which 13 were waited for; matrix products, arithmetic and copies ran while one was open for 4% of the time, Pallas kernels for 10%

profile of v1, /device:TPU:0, one launch (start us, length us, event | category | flops | bytes accessed | tf_op | source)
XLA Modules:
  0.0 711.2 jit_solution(17173801327911562226)
XLA Ops:
  8.8 5.2 convert_element_type.81.wb
  14.7 98.8 %shard_map.152 = (bf16[1024,768]{1,0:T(8,128)(2,1)}, bf16[1024,768]{1,0:T(8,128)(2,1)}, f32[4,9344]{1,0:T(4,128)}, bf16[2,4,768,2304]{3,2,1,0:T(8,128)(2,1)}) custom-call(bf16[256,768]{1,0:T(8,128)(2,1)} %bitcast.75, bf16[256,768]{1,0:T(8,128)(2,1)} %bitcast.77, f32[4,9344]{1,0:T(4,128)} %concatenate.3.meta, bf16[2,384,2304]{2,1,0:T(8,128)(2,1)} %convert_element_type.81.wb), custom_call_target="tpu_custom_call" | custom-call | tf_op jit(solution)/shard_map/pallas_call | solution.py:658
  129.0 5.0 add_select_fusion.1
  138.1 6.6 shard_map.154
  144.7 6.4 shard_map.155
  151.1 14.8 %shard_map.156 = (f32[512,768]{1,0:T(8,128)}, bf16[4,512,768]{2,1,0:T(8,128)(2,1)}, bf16[4,512,768]{2,1,0:T(8,128)(2,1)}) custom-call(s32[1]{0:T(128)} %bitcast.5.flag, f32[512,768]{1,0:T(8,128)} %get-tuple-element.67.x, s32[512,1]{1,0:T(8,128)} %get-tuple-element.151.clip, f32[6,4,768]{2,1,0:T(4,128)} %get-tuple-element.152.mod, ...), custom_call_target="tpu_custom_call" | custom-call | flops 8000000000 | bytes 10000000 | tf_op jit(solution)/shard_map/pallas_call | solution.py:269
  165.9 5.2 shard_map.157
  171.1 17.5 %shard_map.158 = (f32[512,768]{1,0:T(8,128)}, bf16[4,768,768]{2,1,0:T(8,128)(2,1)}) custom-call(s32[1]{0:T(128)} %bitcast.5.flag, f32[512,768]{1,0:T(8,128)} %get-tuple-element.72.g1, f32[512,768]{1,0:T(8,128)} %get-tuple-element.66.x, bf16[4,576,512]{2,1,0:T(8,128)(2,1)} %get-tuple-element.73.qkv_t, bf16[4,192,512]{2,1,0:T(8,128)(2,1)} %get-tuple-element.74.o_t, ...), custom_call_target="tpu_custom_call" | custom-call | flops 16000000000 | bytes 20000000 | tf_op jit(solution)/shard_map/pallas_call | solution.py:269
  189.5 5.2 shard_map.159
  194.7 16.2 %shard_map.160 = (f32[512,768]{1,0:T(8,128)}, bf16[4,768,768]{2,1,0:T(8,128)(2,1)}) custom-call(s32[1]{0:T(128)} %bitcast.5.flag, f32[512,768]{1,0:T(8,128)} %get-tuple-element.79.g1, f32[512,768]{1,0:T(8,128)} %fusion.7.x, bf16[4,576,512]{2,1,0:T(8,128)(2,1)} %get-tuple-element.80.qkv_t, bf16[4,192,512]{2,1,0:T(8,128)(2,1)} %get-tuple-element.81.o_t, ...), custom_call_target="tpu_custom_call" | custom-call | flops 16000000000 | bytes 20000000 | tf_op jit(solution)/shard_map/pallas_call | solution.py:269
  228.5 93.4 %reduce-scatter.9.cloned.1.call-done = bf16[4,384,768]{2,1,0:T(8,128)(2,1)} async-done(((bf16[4,768,768]{2,1,0:T(8,128)(2,1)}), bf16[4,384,768]{2,1,0:T(8,128)(2,1)}) %reduce-scatter.9.cloned.1.call-update) | async-done | bytes 2359312 | tf_op jit(solution)/shard_map/reduce_scatter | solution.py:843
  325.9 17.3 %reduce-scatter.11.cloned.1.call-done = bf16[4,384,1536]{2,1,0:T(8,128)(2,1)} async-done(((bf16[4,768,1536]{2,1,0:T(8,128)(2,1)}), bf16[4,384,1536]{2,1,0:T(8,128)(2,1)}) %reduce-scatter.11.cloned.1.call-update) | async-done | bytes 4718608 | tf_op jit(solution)/shard_map/reduce_scatter | solution.py:843
  350.8 40.2 %collective-permute-done.1 = bf16[256,768]{1,0:T(8,128)(2,1)S(1)} collective-permute-done((bf16[256,768]{1,0:T(8,128)(2,1)}, bf16[256,768]{1,0:T(8,128)(2,1)S(1)}, u32[]{:S(2)}, u32[]{:S(2)}) %collective-permute-start.1) | collective-permute-done | bytes 393248 | tf_op jit(solution)/shard_map/ppermute | solution.py:831
  393.7 46.0 %collective-permute-done.5 = bf16[256,768]{1,0:T(8,128)(2,1)S(1)} collective-permute-done((bf16[256,768]{1,0:T(8,128)(2,1)S(1)}, bf16[256,768]{1,0:T(8,128)(2,1)S(1)}, u32[]{:S(2)}, u32[]{:S(2)}) %collective-permute-start.5) | collective-permute-done | bytes 393248 | tf_op jit(solution)/shard_map/ppermute | solution.py:831
  457.9 43.7 %collective-permute-done.17.ga = bf16[384,1536]{1,0:T(8,128)(2,1)} collective-permute-done((bf16[384,1536]{1,0:T(8,128)(2,1)}, bf16[384,1536]{1,0:T(8,128)(2,1)}, u32[]{:S(2)}, u32[]{:S(2)}) %collective-permute-start.17) | collective-permute-done | bytes 1179680 | tf_op jit(solution)/shard_map/ppermute | solution.py:763
  502.3 9.1 %shard_map.161 = (f32[2,384,2304]{2,1,0:T(8,128)}, f32[2,384,2304]{2,1,0:T(8,128)}, bf16[384,1536]{1,0:T(8,128)(2,1)}) custom-call(s32[1]{0:T(128)} %bitcast.5.flag, f32[2,384,2304]{2,1,0:T(8,128)} %par.15, f32[2,384,2304]{2,1,0:T(8,128)} %bitcast.65, f32[2,384,2304]{2,1,0:T(8,128)} %bitcast.69, bf16[384,1536]{1,0:T(8,128)(2,1)S(1)} %get-tuple-element.130.own, ...), custom_call_target="tpu_custom_call" | custom-call | flops 11796480 | bytes 17694720 | tf_op jit(solution)/shard_map/pallas_call | solution.py:706
  518.0 21.6 %collective-permute-done.11.ga = bf16[384,1536]{1,0:T(8,128)(2,1)} collective-permute-done((bf16[384,1536]{1,0:T(8,128)(2,1)}, bf16[384,1536]{1,0:T(8,128)(2,1)}, u32[]{:S(2)}, u32[]{:S(2)}) %collective-permute-start.11) | collective-permute-done | bytes 1179680 | tf_op jit(solution)/shard_map/ppermute | solution.py:763
  542.1 8.6 %shard_map.163 = (f32[2,384,2304]{2,1,0:T(8,128)}, f32[2,384,2304]{2,1,0:T(8,128)}, bf16[384,1536]{1,0:T(8,128)(2,1)S(1)}) custom-call(s32[1]{0:T(128)} %bitcast.5.flag, f32[2,384,2304]{2,1,0:T(8,128)} %par.15, f32[2,384,2304]{2,1,0:T(8,128)} %bitcast.67, f32[2,384,2304]{2,1,0:T(8,128)} %bitcast.71, ...), custom_call_target="tpu_custom_call", output_to_operand_aliasing={{0}: (8, {}), {1}: (9, {})} | custom-call | flops 11796480 | bytes 17694720 | tf_op jit(solution)/shard_map/pallas_call | solution.py:706
  558.7 61.2 %collective-permute-done.27.rest_2_ = bf16[384,768]{1,0:T(8,128)(2,1)S(1)} collective-permute-done((bf16[384,768]{1,0:T(8,128)(2,1)S(1)}, bf16[384,768]{1,0:T(8,128)(2,1)S(1)}, u32[]{:S(2)}, u32[]{:S(2)}) %collective-permute-start.27) | collective-permute-done | bytes 589856 | tf_op jit(solution)/shard_map/ppermute | solution.py:854
  622.2 22.9 %collective-permute-done.26.rest_1_ = bf16[384,768]{1,0:T(8,128)(2,1)S(1)} collective-permute-done((bf16[384,768]{1,0:T(8,128)(2,1)S(1)}, bf16[384,768]{1,0:T(8,128)(2,1)S(1)}, u32[]{:S(2)}, u32[]{:S(2)}) %collective-permute-start.26) | collective-permute-done | bytes 589856 | tf_op jit(solution)/shard_map/ppermute | solution.py:854
  664.5 9.2 %shard_map.165 = (f32[2,384,2304]{2,1,0:T(8,128)}, f32[2,384,2304]{2,1,0:T(8,128)}, f32[2,384,2304]{2,1,0:T(8,128)}, bf16[2,384,2304]{2,1,0:T(8,128)(2,1)}) custom-call(f32[2,384,2304]{2,1,0:T(8,128)} %par.15, f32[2,384,2304]{2,1,0:T(8,128)} %mom.7, bf16[384,1536]{1,0:T(8,128)(2,1)} %get-tuple-element.99.rest_0_, ...), custom_call_target="tpu_custom_call" | custom-call | flops 11796480 | bytes 17694720 | tf_op jit(solution)/shard_map/pallas_call | solution.py:748
  678.0 8.6 %shard_map.167 = (f32[2,384,2304]{2,1,0:T(8,128)}, f32[2,384,2304]{2,1,0:T(8,128)}, f32[2,384,2304]{2,1,0:T(8,128)}, bf16[2,384,2304]{2,1,0:T(8,128)(2,1)}) custom-call(f32[2,384,2304]{2,1,0:T(8,128)} %par.15, f32[2,384,2304]{2,1,0:T(8,128)} %mom.7, ...), custom_call_target="tpu_custom_call", output_to_operand_aliasing={{0}: (6, {}), {1}: (7, {}), {2}: (8, {}), {3}: (9, {})} | custom-call | flops 11796480 | bytes 17694720 | tf_op jit(solution)/shard_map/pallas_call | solution.py:748
  689.0 10.4 %collective-permute-done.21.rest_2_ = bf16[384,768]{1,0:T(8,128)(2,1)} collective-permute-done((bf16[384,768]{1,0:T(8,128)(2,1)}, bf16[384,768]{1,0:T(8,128)(2,1)}, u32[]{:S(2)}, u32[]{:S(2)}) %collective-permute-start.21) | collective-permute-done | bytes 589856 | tf_op jit(solution)/shard_map/ppermute | solution.py:854
  699.8 4.7 shard_map.168
  (161 shorter events, 119.1 us)
Async XLA Ops:
  7.2 314.7 %reduce-scatter.9.cloned.1.call-start = ((), (), s32[]{:S(2)}) async-start(), calls=%async_computation.6 | async-start | bytes 7077888 | tf_op jit(solution)/shard_map/reduce_scatter | solution.py:843
  188.7 154.5 %reduce-scatter.11.cloned.1.call-start = ((), (), s32[]{:S(2)}) async-start(), calls=%async_computation.7 | async-start | bytes 14155776 | tf_op jit(solution)/shard_map/reduce_scatter | solution.py:843
  189.4 255.4 %reduce-scatter.7.cloned.1.call-start = ((), (), s32[]{:S(2)}) async-start(), calls=%async_computation.5 | async-start | bytes 14155776 | tf_op jit(solution)/shard_map/reduce_scatter | solution.py:843
  194.7 260.1 %reduce-scatter.5.cloned.1.call-start = ((), (), s32[]{:S(2)}) async-start(), calls=%async_computation.4 | async-start | bytes 7077888 | tf_op jit(solution)/shard_map/reduce_scatter | solution.py:843
  222.9 168.1 %collective-permute-start.1 = (bf16[256,768]{1,0:T(8,128)(2,1)}, bf16[256,768]{1,0:T(8,128)(2,1)S(1)}, u32[]{:S(2)}, u32[]{:S(2)}) collective-permute-start(bf16[256,768]{1,0:T(8,128)(2,1)} %get-tuple-element.146), channel_id=1, source_target_pairs={{1,0},{6,7},{9,8},{14,15},{17,16},{22,23},{25,24},{30,31}} | collective-permute-start | bytes 1179656 | tf_op jit(solution)/shard_map/ppermute | solution.py:831
  224.2 168.1 %collective-permute-start.3 = (bf16[256,768]{1,0:T(8,128)(2,1)}, bf16[256,768]{1,0:T(8,128)(2,1)}, u32[]{:S(2)}, u32[]{:S(2)}) collective-permute-start(bf16[256,768]{1,0:T(8,128)(2,1)} %get-tuple-element.147), channel_id=1, source_target_pairs={{1,3},{6,4},{9,11},{14,12},{17,19},{22,20},{25,27},{30,28}} | collective-permute-start | bytes 1179656 | tf_op jit(solution)/shard_map/ppermute | solution.py:831
  225.6 167.4 %collective-permute-start.2 = (bf16[256,768]{1,0:T(8,128)(2,1)}, bf16[256,768]{1,0:T(8,128)(2,1)}, u32[]{:S(2)}, u32[]{:S(2)}) collective-permute-start(bf16[256,768]{1,0:T(8,128)(2,1)} %get-tuple-element.148), channel_id=1, source_target_pairs={{1,2},{6,5},{9,10},{14,13},{17,18},{22,21},{25,26},{30,29}} | collective-permute-start | bytes 1179656 | tf_op jit(solution)/shard_map/ppermute | solution.py:831
  324.6 118.1 %collective-permute-start.16 = (bf16[384,768]{1,0:T(8,128)(2,1)S(1)}, bf16[384,768]{1,0:T(8,128)(2,1)S(1)}, u32[]{:S(2)}, u32[]{:S(2)}) collective-permute-start(bf16[384,768]{1,0:T(8,128)(2,1)S(1)} %get-tuple-element.135), channel_id=1, source_target_pairs={{1,3},{2,0},{5,7},{6,4},{9,11},{10,8},{13,15},{14,12},{17,19},{18,... | collective-permute-start | bytes 1769480 | tf_op jit(solution)/shard_map/ppermute | solution.py:763
  347.4 106.1 %collective-permute-start.19 = (bf16[384,1536]{1,0:T(8,128)(2,1)}, bf16[384,1536]{1,0:T(8,128)(2,1)}, u32[]{:S(2)}, u32[]{:S(2)}) collective-permute-start(bf16[384,1536]{1,0:T(8,128)(2,1)} %get-tuple-element.127), channel_id=1, source_target_pairs={{1,3},{2,0},{5,7},{6,4},{9,11},{10,8},{13,15},{14,12},{17,19},{18,... | collective-permute-start | bytes 3538952 | tf_op jit(solution)/shard_map/ppermute | solution.py:763
  391.0 48.7 %collective-permute-start.5 = (bf16[256,768]{1,0:T(8,128)(2,1)S(1)}, bf16[256,768]{1,0:T(8,128)(2,1)S(1)}, u32[]{:S(2)}, u32[]{:S(2)}) collective-permute-start(bf16[256,768]{1,0:T(8,128)(2,1)S(1)} %get-tuple-element.143), channel_id=1, source_target_pairs={{1,0},{6,7},{9,8},{14,15},{17,16},{22,23},{25,24},{30,31}} | collective-permute-start | bytes 1179656 | tf_op jit(solution)/shard_map/ppermute | solution.py:831
  392.3 48.7 %collective-permute-start.7 = (bf16[256,768]{1,0:T(8,128)(2,1)S(1)}, bf16[256,768]{1,0:T(8,128)(2,1)S(1)}, u32[]{:S(2)}, u32[]{:S(2)}) collective-permute-start(bf16[256,768]{1,0:T(8,128)(2,1)S(1)} %get-tuple-element.144), channel_id=1, source_target_pairs={{1,3},{6,4},{9,11},{14,12},{17,19},{22,20},{25,27},{30,28}} | collective-permute-start | bytes 1179656 | tf_op jit(solution)/shard_map/ppermute | solution.py:831
  393.0 56.1 %collective-permute-start.15 = (bf16[384,768]{1,0:T(8,128)(2,1)}, bf16[384,768]{1,0:T(8,128)(2,1)S(1)}, u32[]{:S(2)}, u32[]{:S(2)}) collective-permute-start(bf16[384,768]{1,0:T(8,128)(2,1)} %get-tuple-element.136), channel_id=1, source_target_pairs={{1,2},{2,1},{5,6},{6,5},{9,10},{10,9},{13,14},{14,13},{17,18},{18,... | collective-permute-start | bytes 1769480 | tf_op jit(solution)/shard_map/ppermute | solution.py:763
  443.6 58.0 %collective-permute-start.17 = (bf16[384,1536]{1,0:T(8,128)(2,1)}, bf16[384,1536]{1,0:T(8,128)(2,1)}, u32[]{:S(2)}, u32[]{:S(2)}) collective-permute-start(bf16[384,1536]{1,0:T(8,128)(2,1)} %get-tuple-element.129), channel_id=1, source_target_pairs={{1,0},{2,3},{5,4},{6,7},{9,8},{10,11},{13,12},{14,15},{17,16},{18,... | collective-permute-start | bytes 3538952 | tf_op jit(solution)/shard_map/ppermute | solution.py:763
  449.9 66.0 %collective-permute-start.13 = (bf16[384,1536]{1,0:T(8,128)(2,1)}, bf16[384,1536]{1,0:T(8,128)(2,1)}, u32[]{:S(2)}, u32[]{:S(2)}) collective-permute-start(bf16[384,1536]{1,0:T(8,128)(2,1)} %get-tuple-element.131), channel_id=1, source_target_pairs={{1,3},{2,0},{5,7},{6,4},{9,11},{10,8},{13,15},{14,12},{17,19},{18,... | collective-permute-start | bytes 3538952 | tf_op jit(solution)/shard_map/ppermute | solution.py:763
  451.8 64.8 %collective-permute-start.12 = (bf16[384,1536]{1,0:T(8,128)(2,1)}, bf16[384,1536]{1,0:T(8,128)(2,1)}, u32[]{:S(2)}, u32[]{:S(2)}) collective-permute-start(bf16[384,1536]{1,0:T(8,128)(2,1)} %get-tuple-element.132), channel_id=1, source_target_pairs={{1,2},{2,1},{5,6},{6,5},{9,10},{10,9},{13,14},{14,13},{17,18},{18,... | collective-permute-start | bytes 3538952 | tf_op jit(solution)/shard_map/ppermute | solution.py:763
  453.5 86.0 %collective-permute-start.11 = (bf16[384,1536]{1,0:T(8,128)(2,1)}, bf16[384,1536]{1,0:T(8,128)(2,1)}, u32[]{:S(2)}, u32[]{:S(2)}) collective-permute-start(bf16[384,1536]{1,0:T(8,128)(2,1)} %get-tuple-element.133), channel_id=1, source_target_pairs={{1,0},{2,3},{5,4},{6,7},{9,8},{10,11},{13,12},{14,15},{17,16},{18,... | collective-permute-start | bytes 3538952 | tf_op jit(solution)/shard_map/ppermute | solution.py:763
  456.6 94.6 %collective-permute-start.10 = (bf16[384,768]{1,0:T(8,128)(2,1)S(1)}, bf16[384,768]{1,0:T(8,128)(2,1)S(1)}, u32[]{:S(2)}, u32[]{:S(2)}) collective-permute-start(bf16[384,768]{1,0:T(8,128)(2,1)S(1)} %get-tuple-element.139), channel_id=1, source_target_pairs={{1,3},{2,0},{5,7},{6,4},{9,11},{10,8},{13,15},{14,12},{17,19},{18,... | collective-permute-start | bytes 1769480 | tf_op jit(solution)/shard_map/ppermute | solution.py:763
  501.6 49.1 %collective-permute-start.6 = (bf16[256,768]{1,0:T(8,128)(2,1)}, bf16[256,768]{1,0:T(8,128)(2,1)S(1)}, u32[]{:S(2)}, u32[]{:S(2)}) collective-permute-start(bf16[256,768]{1,0:T(8,128)(2,1)} %get-tuple-element.145), channel_id=1, source_target_pairs={{1,2},{6,5},{9,10},{14,13},{17,18},{22,21},{25,26},{30,29}} | collective-permute-start | bytes 1179656 | tf_op jit(solution)/shard_map/ppermute | solution.py:831
  550.7 69.1 %collective-permute-start.27 = (bf16[384,768]{1,0:T(8,128)(2,1)S(1)}, bf16[384,768]{1,0:T(8,128)(2,1)S(1)}, u32[]{:S(2)}, u32[]{:S(2)}) collective-permute-start(bf16[384,768]{1,0:T(8,128)(2,1)S(1)} %get-tuple-element.98.rest_0_), channel_id=1, source_target_pairs={{0,16},{8,24},{16,0},{24,8},{1,17},{9,25},{17,1},{25,9},{2,18},{10... | collective-permute-start | bytes 1769480 | tf_op jit(solution)/shard_map/ppermute | solution.py:854
  552.0 94.4 %collective-permute-start.25 = (bf16[384,1536]{1,0:T(8,128)(2,1)S(1)}, bf16[384,1536]{1,0:T(8,128)(2,1)S(1)}, u32[]{:S(2)}, u32[]{:S(2)}) collective-permute-start(bf16[384,1536]{1,0:T(8,128)(2,1)S(1)} %get-tuple-element.97.rest_0_), channel_id=1, source_target_pairs={{0,24},{8,16},{16,8},{24,0},{1,25},{9,17},{17,9},{25,1},{2,26},{10... | collective-permute-start | bytes 3538952 | tf_op jit(solution)/shard_map/ppermute | solution.py:854
  554.4 101.1 %collective-permute-start.31 = (bf16[384,1536]{1,0:T(8,128)(2,1)}, bf16[384,1536]{1,0:T(8,128)(2,1)}, u32[]{:S(2)}, u32[]{:S(2)}) collective-permute-start(bf16[384,1536]{1,0:T(8,128)(2,1)} %get-tuple-element.99.rest_0_), channel_id=1, source_target_pairs={{0,24},{8,16},{16,8},{24,0},{1,25},{9,17},{17,9},{25,1},{2,26},{10... | collective-permute-start | bytes 3538952 | tf_op jit(solution)/shard_map/ppermute | solution.py:854
  556.6 100.6 %collective-permute-start.30 = (bf16[384,1536]{1,0:T(8,128)(2,1)}, bf16[384,1536]{1,0:T(8,128)(2,1)}, u32[]{:S(2)}, u32[]{:S(2)}) collective-permute-start(bf16[384,1536]{1,0:T(8,128)(2,1)} %get-tuple-element.99.rest_0_), channel_id=1, source_target_pairs={{0,16},{8,24},{16,0},{24,8},{1,17},{9,25},{17,1},{25,9},{2,18},{10... | collective-permute-start | bytes 3538952 | tf_op jit(solution)/shard_map/ppermute | solution.py:854
  558.2 99.5 %collective-permute-start.29 = (bf16[384,1536]{1,0:T(8,128)(2,1)}, bf16[384,1536]{1,0:T(8,128)(2,1)}, u32[]{:S(2)}, u32[]{:S(2)}) collective-permute-start(bf16[384,1536]{1,0:T(8,128)(2,1)} %get-tuple-element.99.rest_0_), channel_id=1, source_target_pairs={{0,8},{8,0},{16,24},{24,16},{1,9},{9,1},{17,25},{25,17},{2,10},{10... | collective-permute-start | bytes 3538952 | tf_op jit(solution)/shard_map/ppermute | solution.py:854
  657.2 42.2 %collective-permute-start.21 = (bf16[384,768]{1,0:T(8,128)(2,1)}, bf16[384,768]{1,0:T(8,128)(2,1)}, u32[]{:S(2)}, u32[]{:S(2)}) collective-permute-start(bf16[384,768]{1,0:T(8,128)(2,1)} %get-tuple-element.96.rest_0_), channel_id=1, source_target_pairs={{0,16},{8,24},{16,0},{24,8},{1,17},{9,25},{17,1},{25,9},{2,18},{10... | collective-permute-start | bytes 1769480 | tf_op jit(solution)/shard_map/ppermute | solution.py:854
  (39 other events, 582.4 us)
Sparse Core Ops, SparseCore 0:
  188.8 133.0 reduce-scatter.8
  324.3 18.9 reduce-scatter.10
  345.7 19.1 reduce-scatter.6
  367.7 13.8 reduce-scatter.4

commit v2 on v1

--- a/solution.py
+++ b/solution.py
@@ -73,7 +73,7 @@
     return copies
 
 
-def attn_fwd(layer, flag, x, clip, idc, idr, mod, w_hbm, x1, qkv_t, o_t, lse, buf, u_s, acc, sems):
+def attn_fwd(layer, flag, x, clip, idc, idr, mod, w_hbm, x1, qo, lse, buf, u_s, acc, sems):
     @pl.when(flag[0] == 1)
     def _():
         width = buf.shape[2]
@@ -89,14 +89,14 @@
         for slot in range(4):
             copies[slot].wait()
             part = mm(u_s[...], buf[slot, :, : 3 * hw], 1, 0)
-            qkv_t[slot] = part.T.astype(bf16)
+            qo[slot, : 3 * hw] = part.T.astype(bf16)
 
             def head_step(head, carry):
                 base = pl.multiple_of(head * HD, HD)
-                keys = qkv_t[slot, pl.ds(hw + base, HD), :].T
-                value_t = qkv_t[slot, pl.ds(2 * hw + base, HD), :]
+                keys = qo[slot, pl.ds(hw + base, HD), :].T
+                value_t = qo[slot, pl.ds(2 * hw + base, HD), :]
                 for q0 in range(0, ROWS, 256):
-                    query_t = qkv_t[slot, pl.ds(base, HD), q0 : q0 + 256]
+                    query_t = qo[slot, pl.ds(base, HD), q0 : q0 + 256]
                     scores = mm(keys, query_t * jnp.asarray(0.125, bf16), 1, 0)
                     allowed = idc[...] == idr[:, q0 : q0 + 256]
                     scores = jnp.where(allowed, scores, neg_fill)
@@ -104,20 +104,20 @@
                     raw = jnp.exp(scores - top)
                     total = jnp.sum(raw, axis=0, keepdims=True)
                     probs = (raw / total).astype(bf16)
-                    o_t[slot, pl.ds(base, HD), q0 : q0 + 256] = mm(value_t, probs, 1, 0).astype(
+                    qo[slot, pl.ds(3 * hw + base, HD), q0 : q0 + 256] = mm(value_t, probs, 1, 0).astype(
                         bf16
                     )
                     lse[slot * heads + head, :, q0 : q0 + 256] = top + jnp.log(total)
                 return carry
 
             lax.fori_loop(0, heads, head_step, 0)
-            acc[...] += mm(buf[slot, :, 3 * hw :], o_t[slot], 1, 0)
+            acc[...] += mm(buf[slot, :, 3 * hw :], qo[slot, 3 * hw :], 1, 0)
         for rows in chunks():
             gate = row_mod(clip[rows, :], mod[2])
             x1[rows, :] = x[rows, :] + gate * acc[:, rows].T
 
 
-def mlp_fwd(layer, flag, x, clip, mod, w_hbm, x2, act, dgelu, buf, u_s, acc, sems):
+def mlp_fwd(layer, flag, x, clip, mod, w_hbm, x2, ad, buf, u_s, acc, sems):
     @pl.when(flag[0] == 1)
     def _():
         half = buf.shape[2] // 2
@@ -135,118 +135,12 @@
                 hid = mm(u_s[rows, :], buf[slot, :, :half], 1, 0)
                 cdf = 0.5 * (1.0 + lax.erf(hid * 0.7071067811865476))
                 pdf = jnp.exp(-0.5 * hid * hid) * 0.3989422804014327
-                act[slot, rows, :] = (hid * cdf).astype(bf16)
-                dgelu[slot, rows, :] = (cdf + hid * pdf).astype(bf16)
-            acc[...] += mm(act[slot], buf[slot, :, half:], 1, 1)
+                ad[slot, 0, rows, :] = (hid * cdf).astype(bf16)
+                ad[slot, 1, rows, :] = (cdf + hid * pdf).astype(bf16)
+            acc[...] += mm(ad[slot, 0], buf[slot, :, half:], 1, 1)
         for rows in chunks():
             gate = row_mod(clip[rows, :], mod[5])
             x2[rows, :] = x[rows, :] + gate * acc[rows, :]
-
-
-def mlp_bwd(
-    layer, flag, g, x, act, dgelu, clip, mod, w_hbm, g1, gw, buf, u_t, d_s, d_t, dh, acc, out, sems, osem
-):
-    @pl.when(flag[0] == 1)
-    def _():
-        half = buf.shape[2] // 2
-        attn_width = w_hbm.shape[3] - 2 * half
-        copies = fetch(w_hbm, buf, sems, layer, attn_width, w_hbm.shape[3])
-        for rows in chunks():
-            normed, _ = moments(x[rows, :])
-            shift = row_mod(clip[rows, :], mod[3])
-            scale = row_mod(clip[rows, :], mod[4])
-            u_t[:, rows] = (normed * (1.0 + scale) + shift).T.astype(bf16)
-            gate = row_mod(clip[rows, :], mod[5])
-            down = gate * g[rows, :]
-            d_s[rows, :] = down.astype(bf16)
-            d_t[:, rows] = down.T.astype(bf16)
-        acc[...] = jnp.zeros_like(acc)
-        sends = []
-        for slot in range(4):
-            copies[slot].wait()
-            if slot >= 2:
-                sends[slot - 2].wait()
-            place = slot % 2
-            for rows in chunks():
-                dact = mm(d_s[rows, :], buf[slot, :, half:], 1, 0)
-                dh[rows, :] = (dact * dgelu[slot, rows, :].astype(f32)).astype(bf16)
-            out[place, :, :half] = mm(u_t[...], dh[...], 1, 0).astype(bf16)
-            out[place, :, half:] = mm(d_t[...], act[slot], 1, 0).astype(bf16)
-            sends.append(pltpu.make_async_copy(out.at[place], gw.at[slot], osem.at[place]))
-            sends[-1].start()
-            acc[...] += mm(dh[...], buf[slot, :, :half], 1, 1)
-        for rows in chunks():
-            normed, inv_std = moments(x[rows, :])
-            scale = row_mod(clip[rows, :], mod[4])
-            g1[rows, :] = g[rows, :] + norm_back(acc[rows, :] * (1.0 + scale), normed, inv_std)
-        sends[2].wait()
-        sends[3].wait()
-
-
-def attn_bwd(
-    layer, flag, g1, x, qkv_t, o_t, lse, clip, idc, idr, mod, w_hbm, g0, gw,
-    buf, u_t, d_t, dq, do_s, acc, out, sems, osem
-):
-    @pl.when(flag[0] == 1)
-    def _():
-        width = buf.shape[2]
-        heads = 3
-        hw = heads * HD
-        copies = fetch(w_hbm, buf, sems, layer, 0, width)
-        for rows in chunks():
-            normed, _ = moments(x[rows, :])
-            shift = row_mod(clip[rows, :], mod[0])
-            scale = row_mod(clip[rows, :], mod[1])
-            u_t[:, rows] = (normed * (1.0 + scale) + shift).T.astype(bf16)
-            gate = row_mod(clip[rows, :], mod[2])
-            d_t[:, rows] = (gate * g1[rows, :]).T.astype(bf16)
-        acc[...] = jnp.zeros_like(acc)
-        sends = []
-        for slot in range(4):
-            copies[slot].wait()
-            if slot >= 2:
-                sends[slot - 2].wait()
-            place = slot % 2
-            out[place, :, 3 * hw :] = mm(d_t[...], o_t[slot], 1, 1).astype(bf16)
-            do_s[...] = mm(buf[slot, :, 3 * hw :], d_t[...], 0, 0).astype(bf16)
-
-            def head_step(head, carry):
-                base = pl.multiple_of(head * HD, HD)
-                keys_t = qkv_t[slot, pl.ds(hw + base, HD), :]
-                keys = keys_t.T
-                values = qkv_t[slot, pl.ds(2 * hw + base, HD), :].T
-                dk = jnp.zeros((HD, ROWS), f32)
-                dv = jnp.zeros((HD, ROWS), f32)
-                for q0 in range(0, ROWS, 256):
-                    query_t = qkv_t[slot, pl.ds(base, HD), q0 : q0 + 256]
-                    grad_t = do_s[pl.ds(base, HD), q0 : q0 + 256]
-                    scores = mm(keys, query_t * jnp.asarray(0.125, bf16), 1, 0)
-                    allowed = idc[...] == idr[:, q0 : q0 + 256]
-                    probs = jnp.where(
-                        allowed, jnp.exp(scores - lse[slot * heads + head, :, q0 : q0 + 256]), 0.0
-                    )
-                    dv = dv + mm(grad_t, probs.astype(bf16), 1, 1)
-                    dp = mm(values, grad_t, 1, 0)
-                    weighted = probs * dp
-                    delta = jnp.sum(weighted, axis=0, keepdims=True)
-                    ds = (weighted - probs * delta).astype(bf16)
-                    dq[pl.ds(base, HD), q0 : q0 + 256] = (mm(keys_t, ds, 1, 0) * 0.125).astype(bf16)
-                    dk = dk + mm(query_t, ds, 1, 1)
-                dq[pl.ds(hw + base, HD), :] = (dk * 0.125).astype(bf16)
-                dq[pl.ds(2 * hw + base, HD), :] = dv.astype(bf16)
-                return carry
-
-            lax.fori_loop(0, heads, head_step, 0)
-            out[place, :, : 3 * hw] = mm(u_t[...], dq[...], 1, 1).astype(bf16)
-            sends.append(pltpu.make_async_copy(out.at[place], gw.at[slot], osem.at[place]))
-            sends[-1].start()
-            acc[...] += mm(buf[slot, :, : 3 * hw], dq[...], 1, 0)
-        for rows in chunks():
-            normed, inv_std = moments(x[rows, :])
-            scale = row_mod(clip[rows, :], mod[1])
-            g0[rows, :] = g1[rows, :] + norm_back(acc[:, rows].T * (1.0 + scale), normed, inv_std)
-        sends[2].wait()
-        sends[3].wait()
 
 
 def any_spec():
@@ -284,11 +178,10 @@
         (flag, x, clip, idc, idr, mod, w),
         (
             sds((ROWS, D), f32),
-            sds((4, 9 * HD, ROWS), bf16),
-            sds((4, 3 * HD, ROWS), bf16),
+            sds((4, 12 * HD, ROWS), bf16),
             sds((HEADS, 1, ROWS), f32),
         ),
-        (vm_spec(),) * 4,
+        (vm_spec(),) * 3,
         [
             VM((4, D, 12 * HD), bf16),
             VM((ROWS, D), bf16),
@@ -305,8 +198,8 @@
     return local_call(
         partial(mlp_fwd, layer),
         (flag, x, clip, mod, w),
-        (sds((ROWS, D), f32), sds((4, ROWS, unit), bf16), sds((4, ROWS, unit), bf16)),
-        (vm_spec(),) * 3,
+        (sds((ROWS, D), f32), sds((4, 2, ROWS, unit), bf16)),
+        (vm_spec(),) * 2,
         [
             VM((4, D, 2 * unit), bf16),
             VM((ROWS, D), bf16),
@@ -314,51 +207,6 @@
             pltpu.SemaphoreType.DMA((4,)),
         ],
         int(8e9), int(1e7),
-    )
-
-
-def run_mlp_bwd(layer, flag, g, x, act, dgelu, clip, mod, w):
-    sds = jax.ShapeDtypeStruct
-    unit = FF // 4
-    return local_call(
-        partial(mlp_bwd, layer),
-        (flag, g, x, act, dgelu, clip, mod, w),
-        (sds((ROWS, D), f32), sds((4, D, 2 * unit), bf16)),
-        (vm_spec(), any_spec()),
-        [
-            VM((4, D, 2 * unit), bf16),
-            VM((D, ROWS), bf16),
-            VM((ROWS, D), bf16),
-            VM((D, ROWS), bf16),
-            VM((ROWS, unit), bf16),
-            VM((ROWS, D), f32),
-            VM((2, D, 2 * unit), bf16),
-            pltpu.SemaphoreType.DMA((4,)),
-            pltpu.SemaphoreType.DMA((2,)),
-        ],
-        int(16e9), int(2e7),
-    )
-
-
-def run_attn_bwd(layer, flag, g1, x, qkv_t, o_t, lse, clip, idc, idr, mod, w):
-    sds = jax.ShapeDtypeStruct
-    return local_call(
-        partial(attn_bwd, layer),
-        (flag, g1, x, qkv_t, o_t, lse, clip, idc, idr, mod, w),
-        (sds((ROWS, D), f32), sds((4, D, 12 * HD), bf16)),
-        (vm_spec(), any_spec()),
-        [
-            VM((4, D, 12 * HD), bf16),
-            VM((D, ROWS), bf16),
-            VM((D, ROWS), bf16),
-            VM((9 * HD, ROWS), bf16),
-            VM((3 * HD, ROWS), bf16),
-            VM((D, ROWS), f32),
-            VM((2, D, 12 * HD), bf16),
-            pltpu.SemaphoreType.DMA((4,)),
-            pltpu.SemaphoreType.DMA((2,)),
-        ],
-        int(16e9), int(2e7),
     )
 
 
@@ -592,8 +440,6 @@
                 for copy in shares[1]:
                     copy.start()
                 pl.when(is_second)(lambda: route(cot, cot_o, cs, cr).start())
-            if k == 4:
-                spread(1)
             for slot in (1, 2, 3):
                 z_copy(k, slot, at_mp(other_mid)).wait_recv()
                 g_copy(k, slot).start()
@@ -607,6 +453,7 @@
                     g_copy(k - 1, slot).wait_recv()
                     for copy in d_copies(k - 1, slot, False):
                         copy.start()
+        spread(1)
         for slot in (1, 2, 3):
             g_copy(count - 1, slot).wait_recv()
             for copy in d_copies(count - 1, slot, False):
@@ -673,57 +520,497 @@
     )(tok, cot, meta, wb)
 
 
-def adam_kernel(flag, par, mom, var, own, ga, gb, gc, *rest):
-    new_m, new_v, diff = rest[-3:]
-    keep = jnp.where(flag[0] == 1, own[...].astype(f32), 0.0)
-    grad = keep + ga[...].astype(f32) + gb[...].astype(f32) + gc[...].astype(f32)
-    one = beta_one * mom[...] + (1 - beta_one) * grad
-    two = beta_two * var[...] + (1 - beta_two) * grad * grad
-    step = one / (1 - beta_one**STEP) / (jnp.sqrt(two / (1 - beta_two**STEP)) + adam_eps)
-    new_m[...] = one
-    new_v[...] = two
-    diff[...] = (inner_rate * (step + decay_rate * par[...])).astype(bf16)
-
-
-def row_block(rows):
-    return 96 if rows % 96 == 0 else rows
-
-
-def adam(flag, layer, first, width, par, mom, var, parts, prev):
+def share_rows(rows, n_grp):
+    part = rows // n_grp
+    return part if part * n_grp == rows and part % 16 == 0 else rows
+
+
+def back_kernel(
+    n_dp, n_grp,
+    xb, pick_t, g_in, clip, idc, idr, mods, lse, xs_0, xm_0, xs_1, xm_1, qo_0, qo_1, ad_0, ad_1,
+    w_hbm, par, mom, var,
+    recv, avg, mix_o, gin_o,
+    g_s, x_b, w_b, a_b, q_b, u_t, d_s, d_t, dh, dq, do_s, acc, out, inbox, st_m, st_a, st_0m, st_0a,
+    p_b, p_in, opt, gsum, diff, box, own_avg,
+    xsem, wsem, asem, ce_s, ce_r, os_s, os_r, loc, pe_s, pe_r, ro_s, ro_r, rl, osem,
+    as_s, as_r, bs_s, bs_r, bl,
+):
+    grp, dp, mp = lax.axis_index("grp"), lax.axis_index("dp"), lax.axis_index("mp")
     rows, cols = par.shape[1], par.shape[2]
-    block = row_block(rows)
+    quarter = mix_o.shape[0]
+    share = share_rows(rows, n_grp)
+    star = 1 + lax.rem(dp, 2)
+    is_mid = jnp.logical_or(mp == 1, mp == 2)
+    is_outer = jnp.logical_not(is_mid)
+    is_main = mp == star
+    is_second = jnp.logical_and(is_mid, mp != star)
+    other_mid = 3 - mp
+    near_outer = jnp.where(mp == 1, 0, 3)
+    far_outer = 3 - near_outer
+    heads = 3
+    hw = heads * HD
+    xs, qo, ad = (xs_0, xm_0, xs_1, xm_1), (qo_0, qo_1), (ad_0, ad_1)
+    mate = (grp, flip(dp, 1), mp)
+    barrier = pltpu.get_barrier_semaphore()
+
+    def at_mp(where):
+        return (grp, dp, where)
+
+    def at_grp(step):
+        return (lax.rem(grp + step, n_grp), dp, mp)
+
+    def at_dp(step):
+        return (grp, lax.rem(dp + step, n_dp), mp)
+
+    def greet(devices):
+        for device in devices:
+            pl.semaphore_signal(barrier, inc=1, device_id=device, device_id_type=MESH_ID)
+        pl.semaphore_wait(barrier, len(devices))
+
+    peers = [at_grp(step) for step in range(1, n_grp)]
+
+    @pl.when(is_mid)
+    def _():
+        greet(
+            [at_mp(0), at_mp(3), at_mp(other_mid)] + peers + [at_dp(step) for step in range(1, n_dp)]
+        )
+
+    @pl.when(is_outer)
+    def _():
+        greet([at_mp(1), at_mp(2)] + peers)
+
+    def remote(src, dst, send, receive, device):
+        return pltpu.make_async_remote_copy(
+            src_ref=src, dst_ref=dst, send_sem=send, recv_sem=receive,
+            device_id=device, device_id_type=MESH_ID,
+        )
+
+    def layer_of(sub):
+        return 1 - sub // 2
+
+    def width_of(sub):
+        return 2 * D if sub % 2 == 0 else D
+
+    def cols_of(sub):
+        return slice(D, cols) if sub % 2 == 0 else slice(0, D)
+
+    def slot_of(step):
+        return 3 - step % 4
+
+    def stage(step):
+        sub, slot = step // 4, slot_of(step)
+        if slot == 0:
+            return st_0m if sub % 2 == 0 else st_0a
+        return (st_m if sub % 2 == 0 else st_a).at[layer_of(sub), slot - 1]
+
+    def loads(step):
+        sub, slot, place = step // 4, slot_of(step), step % 2
+        layer, width = layer_of(sub), width_of(sub)
+        result = [
+            pltpu.make_async_copy(
+                w_hbm.at[layer, slot, :, cols_of(sub)], w_b.at[place, :, :width], wsem.at[place]
+            )
+        ]
+        if sub % 2 == 0:
+            result.append(pltpu.make_async_copy(ad[layer].at[slot], a_b.at[place], asem.at[place]))
+        else:
+            result.append(pltpu.make_async_copy(qo[layer].at[slot], q_b.at[place], asem.at[place]))
+        return result
+
+    def x_load(sub):
+        source = xs[2 * layer_of(sub) + (1 if sub % 2 == 0 else 0)]
+        return pltpu.make_async_copy(source, x_b.at[sub % 2], xsem.at[sub % 2])
+
+    def exchange(step, arrive):
+        width, place = width_of(step // 4), step % 2
+        result = []
+        for hop in range(1, n_dp):
+            target = lax.rem(dp + hop, n_dp)
+            result.append(
+                remote(
+                    out.at[place, pl.ds(pl.multiple_of(target * rows, rows), rows), :width],
+                    inbox.at[place, hop - 1, :, :width],
+                    ce_s.at[step, hop - 1], ce_r.at[step, hop - 1], at_dp(hop),
+                )
+            )
+        return result
+
+    def to_owner(step, slot):
+        sub = step // 4
+        plane = 1 if slot >= 2 else 0
+        place = recv.at[plane, layer_of(sub), :, cols_of(sub)]
+        if slot == 0:
+            return pltpu.make_async_copy(stage(step), place, loc.at[sub])
+        device = at_mp((None, near_outer, other_mid, far_outer)[slot])
+        return remote(stage(step), place, os_s.at[step], os_r.at[sub, plane], device)
+
+    def owner_arrival(sub, plane):
+        place = recv.at[plane, layer_of(sub), :, cols_of(sub)]
+        return remote(place, place, os_s.at[0], os_r.at[sub, plane], mate)
+
+    def finish(step):
+        width, place = width_of(step // 4), step % 2
+        for copy in exchange(step, True):
+            copy.wait_recv()
+        target = stage(step)
+        block = 96 if rows % 96 == 0 else rows
+        for at in range(0, rows, block):
+            mine = pl.ds(pl.multiple_of(dp * rows + at, 16), block)
+            total = out[place, mine, :width].astype(f32)
+            for hop in range(1, n_dp):
+                total = total + inbox[place, hop - 1, at : at + block, :width].astype(f32)
+            target[at : at + block, :] = total.astype(bf16)
+        for copy in exchange(step, False):
+            copy.wait_send()
+        to_owner(step, slot_of(step)).start()
+
+    def put_rows(which, values):
+        for at in range(0, CAP, 256):
+            p_b[at : at + 256, :] = mm(pick_t[at : at + 256, :], values, 1, 0).astype(bf16)
+
+        @pl.when(is_second)
+        def _():
+            remote(p_b, p_in, pe_s.at[which], pe_r.at[which], mate).start()
+
+    def quarter_of(index):
+        return pl.ds(pl.multiple_of(index * quarter, quarter), quarter)
+
+    def row_copies(which, dest):
+        return [
+            remote(
+                p_b.at[quarter_of(index)], dest, ro_s.at[which, turn], ro_r.at[which], at_mp(index)
+            )
+            for turn, index in enumerate((other_mid, 0, 3))
+        ]
+
+    def send_rows(which, dest):
+        @pl.when(is_main)
+        def _():
+            remote(p_b, p_in, pe_s.at[which], pe_r.at[which], mate).wait_recv()
+            for at in range(0, CAP, 256):
+                span = slice(at, at + 256)
+                p_b[span, :] = p_b[span, :] + p_in[span, :]
+            for copy in row_copies(which, dest):
+                copy.start()
+            pltpu.make_async_copy(p_b.at[quarter_of(mp)], dest, rl.at[which]).start()
+
+    def end_rows(which, dest):
+        @pl.when(is_main)
+        def _():
+            for copy in row_copies(which, dest):
+                copy.wait_send()
+            pltpu.make_async_copy(p_b.at[quarter_of(mp)], dest, rl.at[which]).wait()
+
+        @pl.when(is_second)
+        def _():
+            remote(p_b, p_in, pe_s.at[which], pe_r.at[which], mate).wait_send()
+
+    def rows_arrived(which, dest):
+        @pl.when(jnp.logical_not(is_main))
+        def _():
+            remote(
+                p_b.at[quarter_of(0)], dest, ro_s.at[which, 0], ro_r.at[which], at_mp(0)
+            ).wait_recv()
+
+    def piece_place(piece):
+        layer, at = piece
+        return layer, slice(at, at + PIECE), layer * (cols // PIECE) + at // PIECE
+
+    def diff_piece(piece):
+        layer, span, index = piece_place(piece)
+        block = opt.shape[2]
+
+        def block_loads(turn):
+            part, place = slice(turn * block, (turn + 1) * block), turn % 2
+            return [
+                pltpu.make_async_copy(source.at[layer, part, span], opt.at[place, i], osem.at[place, i])
+                for i, source in enumerate((par, mom, var))
+            ] + [
+                pltpu.make_async_copy(
+                    recv.at[plane, layer, part, span], gsum.at[place, plane], osem.at[place, 3 + plane]
+                )
+                for plane in range(2)
+            ]
+
+        for copy in block_loads(0):
+            copy.start()
+        for turn in range(rows // block):
+            part, place = slice(turn * block, (turn + 1) * block), turn % 2
+            if (turn + 1) * block < rows:
+                for copy in block_loads(turn + 1):
+                    copy.start()
+            for copy in block_loads(turn):
+                copy.wait()
+            grad = gsum[place, 0].astype(f32) + gsum[place, 1].astype(f32)
+            one = beta_one * opt[place, 1] + (1 - beta_one) * grad
+            two = beta_two * opt[place, 2] + (1 - beta_two) * grad * grad
+            step = one / (1 - beta_one**STEP) / (jnp.sqrt(two / (1 - beta_two**STEP)) + adam_eps)
+            diff[index, part, :] = (inner_rate * (step + decay_rate * opt[place, 0])).astype(bf16)
+        for copy in first_copies(index):
+            copy.start()
+
+    def rows_for(where):
+        if share == rows:
+            return slice(0, rows)
+        return pl.ds(pl.multiple_of(where * share, share), share)
+
+    def first_copies(index):
+        return [
+            remote(
+                diff.at[index, rows_for(lax.rem(grp + hop, n_grp))], box.at[index, hop - 1],
+                as_s.at[index, hop - 1], as_r.at[index, hop - 1], at_grp(hop),
+            )
+            for hop in range(1, n_grp)
+        ]
+
+    def second_copies(piece):
+        layer, span, index = piece_place(piece)
+        place = avg.at[layer, rows_for(grp), span]
+        return [
+            remote(own_avg.at[index], place, bs_s.at[index, hop - 1], bs_r.at[index, hop - 1], at_grp(hop))
+            for hop in range(1, n_grp)
+        ]
+
+    def second_arrivals(piece):
+        layer, span, index = piece_place(piece)
+        result = []
+        for hop in range(1, n_grp):
+            source = lax.rem(grp + n_grp - hop, n_grp)
+            place = avg.at[layer, rows_for(source), span]
+            result.append(
+                remote(place, place, bs_s.at[index, hop - 1], bs_r.at[index, hop - 1], at_grp(hop))
+            )
+        return result
+
+    def mean_piece(piece):
+        layer, span, index = piece_place(piece)
+        for copy in first_copies(index):
+            copy.wait_recv()
+        total = diff[index, rows_for(grp), :].astype(f32)
+        for hop in range(1, n_grp):
+            total = total + box[index, hop - 1].astype(f32)
+        own_avg[index] = (total / n_grp).astype(bf16)
+        pltpu.make_async_copy(own_avg.at[index], avg.at[layer, rows_for(grp), span], bl.at[index]).start()
+        if share != rows:
+            for copy in second_copies(piece):
+                copy.start()
+
+    def end_piece(piece):
+        layer, span, index = piece_place(piece)
+        for copy in first_copies(index):
+            copy.wait_send()
+        pltpu.make_async_copy(own_avg.at[index], avg.at[layer, rows_for(grp), span], bl.at[index]).wait()
+        if share != rows:
+            for copy in second_copies(piece):
+                copy.wait_send()
+            for copy in second_arrivals(piece):
+                copy.wait_recv()
+
+    def pieces_of(sub):
+        span = cols_of(sub)
+        return [(layer_of(sub), at) for at in range(span.start, span.stop, PIECE)]
+
+    def diffs(sub):
+        @pl.when(is_outer)
+        def _():
+            owner_arrival(sub, 0).wait_recv()
+
+        @pl.when(is_mid)
+        def _():
+            to_owner(4 * sub + 3, 0).wait()
+
+        owner_arrival(sub, 1).wait_recv()
+        for piece in pieces_of(sub):
+            diff_piece(piece)
+
+    def means(sub):
+        for piece in pieces_of(sub):
+            mean_piece(piece)
+
+    def mlp_start(sub):
+        layer, place = layer_of(sub), sub % 2
+        mod = mods.at[layer]
+        x_load(sub).wait()
+        for part in chunks():
+            normed, _ = moments(x_b[place, part, :])
+            shift = row_mod(clip[part, :], mod[3])
+            scale = row_mod(clip[part, :], mod[4])
+            u_t[:, part] = (normed * (1.0 + scale) + shift).T.astype(bf16)
+            down = row_mod(clip[part, :], mod[5]) * g_s[part, :]
+            d_s[part, :] = down.astype(bf16)
+            d_t[:, part] = down.T.astype(bf16)
+        acc[...] = jnp.zeros_like(acc)
+
+    def mlp_step(step):
+        place = step % 2
+        for part in chunks():
+            dact = mm(d_s[part, :], w_b[place, :, D:], 1, 0)
+            dh[part, :] = (dact * a_b[place, 1, part, :].astype(f32)).astype(bf16)
+        out[place, :, :D] = mm(u_t[...], dh[...], 1, 0).astype(bf16)
+        out[place, :, D:] = mm(d_t[...], a_b[place, 0], 1, 0).astype(bf16)
+        acc[...] += mm(w_b[place, :, :D], dh[...], 1, 1)
+
+    def attn_start(sub):
+        layer, place = layer_of(sub), sub % 2
+        mod = mods.at[layer]
+        x_load(sub).wait()
+        for part in chunks():
+            normed, _ = moments(x_b[place, part, :])
+            shift = row_mod(clip[part, :], mod[0])
+            scale = row_mod(clip[part, :], mod[1])
+            u_t[:, part] = (normed * (1.0 + scale) + shift).T.astype(bf16)
+            d_t[:, part] = (row_mod(clip[part, :], mod[2]) * g_s[part, :]).T.astype(bf16)
+        acc[...] = jnp.zeros_like(acc)
+
+    def attn_step(step):
+        layer, place, slot = layer_of(step // 4), step % 2, slot_of(step)
+        out[place, :, 3 * hw : D] = mm(d_t[...], q_b[place, 3 * hw :], 1, 1).astype(bf16)
+        do_s[...] = mm(w_b[place, :, 3 * hw : D], d_t[...], 0, 0).astype(bf16)
+
+        def head_step(head, carry):
+            base = pl.multiple_of(head * HD, HD)
+            keys_t = q_b[place, pl.ds(hw + base, HD), :]
+            keys = keys_t.T
+            values = q_b[place, pl.ds(2 * hw + base, HD), :].T
+            dk = jnp.zeros((HD, ROWS), f32)
+            dv = jnp.zeros((HD, ROWS), f32)
+            for q0 in range(0, ROWS, 256):
+                span = slice(q0, q0 + 256)
+                query_t = q_b[place, pl.ds(base, HD), span]
+                grad_t = do_s[pl.ds(base, HD), span]
+                scores = mm(keys, query_t * jnp.asarray(0.125, bf16), 1, 0)
+                allowed = idc[layer] == idr[layer, :, span]
+                probs = jnp.where(
+                    allowed, jnp.exp(scores - lse[layer, slot * heads + head, :, span]), 0.0
+                )
+                dv = dv + mm(grad_t, probs.astype(bf16), 1, 1)
+                weighted = probs * mm(values, grad_t, 1, 0)
+                delta = jnp.sum(weighted, axis=0, keepdims=True)
+                ds = (weighted - probs * delta).astype(bf16)
+                dq[pl.ds(base, HD), span] = (mm(keys_t, ds, 1, 0) * 0.125).astype(bf16)
+                dk = dk + mm(query_t, ds, 1, 1)
+            dq[pl.ds(hw + base, HD), :] = (dk * 0.125).astype(bf16)
+            dq[pl.ds(2 * hw + base, HD), :] = dv.astype(bf16)
+            return carry
+
+        lax.fori_loop(0, heads, head_step, 0)
+        out[place, :, : 3 * hw] = mm(u_t[...], dq[...], 1, 1).astype(bf16)
+        acc[...] += mm(w_b[place, :, : 3 * hw], dq[...], 1, 0)
+
+    def sub_end(sub):
+        layer, place = layer_of(sub), sub % 2
+        row = 4 if sub % 2 == 0 else 1
+        for part in chunks():
+            normed, inv_std = moments(x_b[place, part, :])
+            scale = row_mod(clip[part, :], mods[layer, row])
+            g_s[part, :] = g_s[part, :] + norm_back(acc[:, part].T * (1.0 + scale), normed, inv_std)
+
+    @pl.when(is_mid)
+    def _():
+        x_load(0).start()
+        for copy in loads(0):
+            copy.start()
+        g_s[...] = g_in[...]
+        put_rows(0, xb[...])
+        for step in range(16):
+            sub = step // 4
+            if step + 1 < 16:
+                for copy in loads(step + 1):
+                    copy.start()
+            if step % 4 == 0:
+                if sub < 3:
+                    x_load(sub + 1).start()
+                (mlp_start if sub % 2 == 0 else attn_start)(sub)
+            for copy in loads(step):
+                copy.wait()
+            (mlp_step if sub % 2 == 0 else attn_step)(step)
+            if step >= 2:
+                finish(step - 1)
+            for copy in exchange(step, True):
+                copy.start()
+            if step == 0:
+                finish(0)
+                send_rows(0, mix_o)
+            if step % 4 == 3:
+                sub_end(sub)
+            if step == 9:
+                diffs(0)
+            if step == 11:
+                means(0)
+            if step == 14:
+                diffs(1)
+        end_rows(0, mix_o)
+        put_rows(1, g_s[...].astype(bf16))
+        finish(15)
+        means(1)
+        send_rows(1, gin_o)
+        diffs(2)
+        means(2)
+        diffs(3)
+        means(3)
+        for step in range(16):
+            if slot_of(step) != 0:
+                to_owner(step, slot_of(step)).wait_send()
+        end_rows(1, gin_o)
+
+    @pl.when(is_outer)
+    def _():
+        for sub in range(4):
+            diffs(sub)
+            means(sub)
+
+    for which, dest in ((0, mix_o), (1, gin_o)):
+        rows_arrived(which, dest)
+    for layer in range(L):
+        for at in range(0, cols, PIECE):
+            end_piece((layer, at))
+
+
+def run_back(xb, pick_t, g, clip, idc, idr, mods, lse, xs, qo, ad, w, par, mom, var, quarter):
     sds = jax.ShapeDtypeStruct
-    base = first // PIECE
-    full = pl.BlockSpec((None, block, PIECE), lambda i, j: (layer, i, base + j))
-    piece = pl.BlockSpec((block, PIECE), lambda i, j: (i, j))
-    ins = [flag, par, mom, var, *parts]
-    specs = [smem_spec(), full, full, full] + [piece] * 4
-    aliases = {}
-    if prev is not None:
-        aliases = {len(ins): 0, len(ins) + 1: 1}
-        ins += list(prev)
-        specs += [any_spec(), any_spec()]
+    n_dp, n_grp = lax.axis_size("dp"), lax.axis_size("grp")
+    rows, cols = par.shape[1], par.shape[2]
+    share = share_rows(rows, n_grp)
+    count = L * cols // PIECE
+    far, peers = n_dp - 1, n_grp - 1
+    block = 96 if rows % 96 == 0 else rows
     return pl.pallas_call(
-        adam_kernel,
-        grid=(rows // block, width // PIECE),
-        out_shape=(sds(par.shape, f32), sds(par.shape, f32), sds((rows, width), bf16)),
-        in_specs=specs,
-        out_specs=(full, full, piece),
-        input_output_aliases=aliases,
-        compiler_params=pltpu.CompilerParams(vmem_limit_bytes=48 * MIB),
-        cost_estimate=pl.CostEstimate(
-            flops=rows * width * 20, bytes_accessed=rows * width * 30, transcendentals=0
+        partial(back_kernel, n_dp, n_grp),
+        out_shape=(
+            sds((2, L, rows, cols), bf16), sds((L, rows, cols), bf16),
+            sds((quarter, D), bf16), sds((quarter, D), bf16),
         ),
-    )(*ins)
-
-
-def outer_kernel(count, par, mom, *rest):
-    total = rest[0][...].astype(f32)
-    for other in rest[1:count]:
-        total = total + other[...].astype(f32)
-    average = total / count
-    out_a, out_m, out_w, out_l = rest[-4:]
-    momentum = outer_mu * mom[...] + average
+        in_specs=[vm_spec()] * 8 + [any_spec()] * 12,
+        out_specs=(any_spec(),) * 4,
+        scratch_shapes=[
+            VM((ROWS, D), f32), VM((2, ROWS, D), f32), VM((2, D, 2 * D), bf16),
+            VM((2, 2, ROWS, D), bf16), VM((2, D, ROWS), bf16),
+            VM((D, ROWS), bf16), VM((ROWS, D), bf16), VM((D, ROWS), bf16), VM((ROWS, D), bf16),
+            VM((9 * HD, ROWS), bf16), VM((3 * HD, ROWS), bf16), VM((D, ROWS), f32),
+            VM((2, D, 2 * D), bf16), VM((2, far, rows, 2 * D), bf16),
+            VM((L, 3, rows, 2 * D), bf16), VM((L, 3, rows, D), bf16),
+            VM((rows, 2 * D), bf16), VM((rows, D), bf16),
+            VM((CAP, D), bf16), VM((CAP, D), bf16),
+            VM((2, 3, block, PIECE), f32), VM((2, 2, block, PIECE), bf16),
+            VM((count, rows, PIECE), bf16), VM((count, peers, share, PIECE), bf16),
+            VM((count, share, PIECE), bf16),
+            DMA((2,)), DMA((2,)), DMA((2,)), DMA((16, far)), DMA((16, far)), DMA((16,)), DMA((4, 2)),
+            DMA((4,)), DMA((2,)), DMA((2,)), DMA((2, 3)), DMA((2,)), DMA((2,)), DMA((2, 5)),
+            DMA((count, peers)), DMA((count, peers)), DMA((count, peers)), DMA((count, peers)),
+            DMA((count,)),
+        ],
+        compiler_params=pltpu.CompilerParams(
+            collective_id=2, has_side_effects=True, vmem_limit_bytes=63 * MIB
+        ),
+    )(xb, pick_t, g, clip, idc, idr, mods, lse, *xs, *qo, *ad, w, par, mom, var)
+
+
+def last_kernel(par, mom, var, out_mom, ga, gb, avg, new_m, new_v, out_a, out_m, out_w, out_l):
+    grad = ga[...].astype(f32) + gb[...].astype(f32)
+    new_m[...] = beta_one * mom[...] + (1 - beta_one) * grad
+    new_v[...] = beta_two * var[...] + (1 - beta_two) * grad * grad
+    average = avg[...].astype(f32)
+    momentum = outer_mu * out_mom[...] + average
     updated = par[...] - outer_rate * (average + outer_mu * momentum)
     out_a[...] = average
     out_m[...] = momentum
@@ -731,47 +1018,32 @@
     out_l[...] = updated.astype(bf16)
 
 
-def outer(layer, first, width, par, mom, diffs, prev):
+def run_last(par, mom, var, out_mom, recv, avg):
     rows, cols = par.shape[1], par.shape[2]
-    block = row_block(rows)
+    block = 96 if rows % 96 == 0 else rows
     sds = jax.ShapeDtypeStruct
-    base = first // PIECE
-    full = pl.BlockSpec((None, block, PIECE), lambda i, j: (layer, i, base + j))
-    piece = pl.BlockSpec((block, PIECE), lambda i, j: (i, j))
-    ins = [par, mom, *diffs]
-    specs = [full, full] + [piece] * len(diffs)
-    aliases = {}
-    if prev is not None:
-        aliases = {len(ins) + i: i for i in range(4)}
-        ins += list(prev)
-        specs += [any_spec()] * 4
+    full = pl.BlockSpec((None, block, cols), lambda i, j: (i, j, 0))
+
+    def plane(which):
+        return pl.BlockSpec((None, None, block, cols), lambda i, j: (which, i, j, 0))
+
     return pl.pallas_call(
-        partial(outer_kernel, len(diffs)),
-        grid=(rows // block, width // PIECE),
-        out_shape=(sds(par.shape, f32),) * 3 + (sds(par.shape, bf16),),
-        in_specs=specs,
-        out_specs=(full,) * 4,
-        input_output_aliases=aliases,
+        last_kernel,
+        grid=(L, rows // block),
+        out_shape=(sds(par.shape, f32),) * 5 + (sds(par.shape, bf16),),
+        in_specs=[full] * 4 + [plane(0), plane(1), full],
+        out_specs=(full,) * 6,
         compiler_params=pltpu.CompilerParams(vmem_limit_bytes=48 * MIB),
-        cost_estimate=pl.CostEstimate(
-            flops=rows * width * 20, bytes_accessed=rows * width * 30, transcendentals=0
-        ),
-    )(*ins)
-
-
-def send_mp(values, pairs):
-    return lax.ppermute(values, "mp", pairs)
+    )(par, mom, var, out_mom, recv, recv, avg)
 
 
 def body(
     tokens, cotangent, modulation, clip_frames, clip_patches, params, first_moment, second_moment,
     outer_momentum,
 ):
-    n_dp = lax.axis_size("dp")
-    n_grp = lax.axis_size("grp")
     dp, mp = lax.axis_index("dp"), lax.axis_index("mp")
     quarter = tokens.shape[1]
-    rows, cols = params.shape[1], params.shape[2]
+    mod_cols = modulation.shape[2]
     star = 1 + lax.rem(dp, 2)
     is_mid = jnp.logical_or(mp == 1, mp == 2)
     flag = is_mid.astype(jnp.int32)[None]
@@ -787,89 +1059,41 @@
     )
     tok_all, cot_all, meta_all, w = gather_all(tokens[0], cotangent[0], meta, params.astype(bf16))
 
-    mods = meta_all[:, : modulation.shape[2]].reshape(SLOTS, L, 6, D).transpose(1, 2, 0, 3)
-    frames = meta_all[:, modulation.shape[2]]
-    patches = meta_all[:, modulation.shape[2] + 1]
+    mods = meta_all[:, :mod_cols].reshape(SLOTS, L, 6, D).transpose(1, 2, 0, 3)
+    frames, patches = meta_all[:, mod_cols], meta_all[:, mod_cols + 1]
     pos, live, clip, space_id, time_id = slot_meta(frames, patches, mp == star)
-    pick = (pos[:, None] == jnp.arange(CAP, dtype=jnp.int32)[None, :]) & live[:, None]
-    pick = pick.astype(bf16)
+    every = jnp.arange(CAP, dtype=jnp.int32)
+    pick = ((pos[:, None] == every[None, :]) & live[:, None]).astype(bf16)
+    pick_t = ((pos[None, :] == every[:, None]) & live[None, :]).astype(bf16)
     clip = clip[:, None]
+    ids = jnp.stack([space_id, time_id])
 
     x = jnp.dot(pick, tok_all, preferred_element_type=f32)
     gradient = jnp.dot(pick, cot_all, preferred_element_type=f32)
-    ids = (space_id, time_id)
-    kept = []
+    xs, qos, ads, lses = [], [], [], []
     for layer in range(L):
-        idc, idr = ids[layer % 2][:, None], ids[layer % 2][None, :]
-        x1, qkv_t, o_t, lse = run_attn_fwd(layer, flag, x, clip, idc, idr, mods[layer], w)
-        x2, act, dgelu = run_mlp_fwd(layer, flag, x1, clip, mods[layer], w)
-        kept.append((x, x1, qkv_t, o_t, lse, act, dgelu))
+        x1, qo, lse = run_attn_fwd(
+            layer, flag, x, clip, ids[layer % 2][:, None], ids[layer % 2][None, :], mods[layer], w
+        )
+        x2, ad = run_mlp_fwd(layer, flag, x1, clip, mods[layer], w)
+        xs += [x, x1]
+        qos.append(qo)
+        ads.append(ad)
+        lses.append(lse)
         x = x2
-
-    back = [
-        [((d, s), (d, o)) for d, s, o in ((d, 1 + d % 2, order(d)) for d in range(n_dp))]
-        for order in (
-            lambda d: 0 if d % 2 == 0 else 3,
-            lambda d: 2 if d % 2 == 0 else 1,
-            lambda d: 3 if d % 2 == 0 else 0,
-        )
-    ]
-    quarters = [jnp.where(star == 1, a, b) for a, b in ((0, 3), (2, 1), (3, 0))]
-    swap = [(d, d ^ 1) for d in range(n_dp)]
-
-    def send_back(values):
-        placed = lax.dot_general(
-            pick, values.astype(bf16), (((0,), (0,)), ((), ())), preferred_element_type=f32
-        ).astype(bf16)
-        placed = jnp.where(is_mid, placed, jnp.zeros_like(placed))
-        placed = placed + lax.ppermute(placed, "dp", swap)
-        mine = lax.dynamic_slice_in_dim(placed, mp * quarter, quarter, 0)
-        result = jnp.where(mp == star, mine, jnp.zeros_like(mine))
-        for pairs, index in zip(back, quarters):
-            piece = lax.dynamic_slice_in_dim(placed, index * quarter, quarter, 0)
-            flat = [(a[0] * 4 + a[1], b[0] * 4 + b[1]) for a, b in pairs]
-            result = result + lax.ppermute(piece, ("dp", "mp"), flat)
-        return result
-
+    recv, avg, mixed_rows, grad_rows = run_back(
+        x.astype(bf16), pick_t, gradient, clip, ids[:, :, None], ids[:, None, :], mods,
+        jnp.stack(lses), xs, qos, ads, w, params, first_moment[0], second_moment[0], quarter,
+    )
     total = jnp.sum(clip_frames[0] * clip_patches[0])
     own_live = (mp * quarter + jnp.arange(quarter, dtype=jnp.int32) < total)[:, None]
-    mixed = jnp.where(own_live, send_back(x), tokens[0])
-
-    mom, var = first_moment[0], second_moment[0]
-    state, done = None, None
-
-    def finish(layer, first, grads, state, done):
-        width = grads.shape[2]
-        share = lax.psum_scatter(grads, "dp", scatter_dimension=1, tiled=True)
-        parts = (
-            share[0],
-            send_mp(share[1], [(1, 0), (2, 3)]),
-            send_mp(share[2], [(1, 2), (2, 1)]),
-            send_mp(share[3], [(1, 3), (2, 0)]),
-        )
-        new_m, new_v, diff = adam(flag, layer, first, width, params, mom, var, parts, state)
-        diffs = [diff] + [
-            lax.ppermute(diff, "grp", [(g, (g + step) % n_grp) for g in range(n_grp)])
-            if n_grp != 4
-            else lax.ppermute(diff, "grp", [(g, g ^ step) for g in range(n_grp)])
-            for step in range(1, n_grp)
-        ]
-        done = outer(layer, first, width, params, outer_momentum, diffs, done)
-        return (new_m, new_v), done
-
-    for layer in reversed(range(L)):
-        idc, idr = ids[layer % 2][:, None], ids[layer % 2][None, :]
-        x0, x1, qkv_t, o_t, lse, act, dgelu = kept[layer]
-        g1, g_mlp = run_mlp_bwd(layer, flag, gradient, x1, act, dgelu, clip, mods[layer], w)
-        state, done = finish(layer, PIECE, g_mlp, state, done)
-        gradient, g_attn = run_attn_bwd(
-            layer, flag, g1, x0, qkv_t, o_t, lse, clip, idc, idr, mods[layer], w
-        )
-        state, done = finish(layer, 0, g_attn, state, done)
-    input_grad = send_back(gradient).astype(f32)
-    average, momentum, updated, low = done
+    mixed = jnp.where(own_live, mixed_rows, tokens[0])
+    input_grad = jnp.where(own_live, grad_rows.astype(f32), 0.0)
+    new_m, new_v, average, momentum, updated, low = run_last(
+        params, first_moment[0], second_moment[0], outer_momentum, recv, avg
+    )
     return (
-        mixed[None], input_grad[None], state[0][None], state[1][None], average, momentum, updated, low,
+        mixed[None], input_grad[None], new_m[None], new_v[None], average, momentum, updated, low,
     )
 
 

time: 719 us -> 497 us (0.69)
  waiting for transfers between devices: 363 us -> 0 us
  Pallas kernels: 228 us -> 448 us
  starting transfers between devices: 37.5 us -> 0 us
  local copies, waits for them, and re-layouts: 30.5 us -> 7.54 us
  between operations: 14.5 us -> 1.34 us
    pallas_call x8 -> x2, Pallas kernels: 53.5 us -> 327 us  [the longest x1 302 us: run_back(): pl.pallas_call(partial(back_kernel, n_dp, n_grp), out_shape=(sds((2, L, r...]
    ppermute x32 -> x0, waiting for transfers between devices: 251 us -> none  [the longest x12 97.3 us: finish(): lax.ppermute(diff, 'grp', [(g, g ^ step) for g in range(n_grp)])]
    reduce_scatter x4 -> x0, waiting for transfers between devices: 111 us -> none  [finish(): share = lax.psum_scatter(grads, 'dp', scatter_dimension=1, tiled=True)]
    pallas_call x8 -> x4, Pallas kernels: 76.1 us -> 22.2 us  [local_call(): pl.pallas_call(kernel, out_shape=outs, in_specs=spaces, out_specs=out_spa...]
    ppermute x32 -> x0, starting transfers between devices: 37.4 us -> none  [the longest x12 15.1 us: send_mp(): return lax.ppermute(values, 'mp', pairs)]
    squeeze x4 -> x0, local copies, waits for them, and re-layouts: 12.9 us -> none  [finish(): share[3]]
    unnamed x54 -> x14, local copies, waits for them, and re-layouts: 11.5 us -> 2.03 us
  transfers between devices with their start and end apart: 36 -> 0, of which waited for: 13 -> 0; matrix products, arithmetic and copies ran while one was open for 4% -> 0% of each run, Pallas kernels for 10% -> 0%
where the time goes in v2:
time: 497 us; the launch traced here: 490 us
  Pallas kernels  448 us (90%)
  other arithmetic  27.2 us (5%)
  local copies, waits for them, and re-layouts  7.54 us (2%)
  matrix products  6.09 us (1%)
    pallas_call x1, Pallas kernels, run_back(): pl.pallas_call(partial(back_kernel, n_dp, n_grp), out_shape=(sds((2, L, r...  302 us
    pallas_call x1, Pallas kernels, gather_all(): pl.pallas_call(partial(gather_kernel, n_dp), out_shape=(sds((CAP, D), bf1...  98.8 us
    pallas_call x1, Pallas kernels, run_last(): pl.pallas_call(last_kernel, grid=(L, rows // block), out_shape=(sds(par.s...  25.2 us
    pallas_call x4, Pallas kernels, local_call(): pl.pallas_call(kernel, out_shape=outs, in_specs=spaces, out_specs=out_spa...  22.2 us

profile of v2, /device:TPU:0, one launch (start us, length us, event | category | flops | bytes accessed | tf_op | source)
XLA Modules:
  0.0 490.0 jit_solution(17187175037990145194)
XLA Ops:
  0.6 1.4 multiply_reduce_fusion
  2.9 1.7 concatenate.3.meta
  4.5 5.1 %convert_element_type.77.wb = bf16[2,384,2304]{2,1,0:T(8,128)(2,1)} convert(f32[2,384,2304]{2,1,0:T(8,128)} %par.3) | non-fusion elementwise | flops 1769472 | bytes 10616832 | tf_op jit(solution)/shard_map/convert_element_type | solution.py:1060
  9.7 98.8 %shard_map.152 = (bf16[1024,768]{1,0:T(8,128)(2,1)}, bf16[1024,768]{1,0:T(8,128)(2,1)}, f32[4,9344]{1,0:T(4,128)}, bf16[2,4,768,2304]{3,2,1,0:T(8,128)(2,1)}) custom-call(bf16[256,768]{1,0:T(8,128)(2,1)} %bitcast.40, bf16[256,768]{1,0:T(8,128)(2,1)} %bitcast.43, f32[4,9344]{1,0:T(4,128)} %concatenate.3.meta, bf16[2,384,2304]{2,1,0:T(8,128)(2,1)} %convert_element_type.77.wb), custom_call_target="tpu_custom_call" | custom-call | tf_op jit(solution)/shard_map/pallas_call | solution.py:505
  108.5 1.0 convert_reduce_fusion.1
  109.5 0.9 slice.19
  111.2 1.3 select_select_fusion
  113.2 3.8 fusion.3.x.xs_0
  117.0 2.3 fusion.1.g_in
  119.4 1.5 add_select_fusion.2
  123.4 5.0 %add_select_fusion.1 = (s32[512,1]{1,0:T(8,128)}, s32[512,1]{1,0:T(8,128)}, s32[512,1]{1,0:T(8,128)}) fusion(s32[512,1]{1,0:T(8,128)S(1)} %copy.35, s32[512,1]{1,0:T(8,128)S(1)} %copy.34, s32[]{:T(128)} %get-tuple-element.60, s32[]{:T(128)} %get-tuple-element.61, pred[]{:T(512)S(6)} %eq.53, s32[512,1]{1,0:T(8,128)S(1)} %copy.32), kind=kLoop, calls=%fused_computation.14 | loop fusion | flops 13824 | bytes 12297 | tf_op jit(solution)/shard_map/jit(_where)/select_n | solution.py:236
  128.4 1.0 copy.39.idc
  129.4 1.4 fusion.6.pick_t
  130.8 3.9 shard_map.153
  134.8 6.8 %shard_map.154 = (f32[512,768]{1,0:T(8,128)}, bf16[4,2,512,768]{3,2,1,0:T(8,128)(2,1)}) custom-call(s32[1]{0:T(128)} %bitcast.flag, f32[512,768]{1,0:T(8,128)} %get-tuple-element.35.x.xm_0, s32[512,1]{1,0:T(8,128)} %get-tuple-element.69.clip, f32[6,4,768]{2,1,0:T(4,128)} %get-tuple-element.71.mod, bf16[2,4,768,2304]{3,2,1,0:T(8,128)(2,1)} %get-tuple-element.34.w_hbm), custom_call_target="tpu_custom_call" | custom-call | flops 8000000000 | bytes 10000000 | tf_op jit(solution)/shard_map/pallas_call | solution.py:163
  141.6 6.2 %shard_map.155 = (f32[512,768]{1,0:T(8,128)}, bf16[4,768,512]{2,1,0:T(8,128)(2,1)}, f32[12,1,512]{2,1,0:T(1,128)}) custom-call(s32[1]{0:T(128)} %bitcast.flag, f32[512,768]{1,0:T(8,128)} %get-tuple-element.36.x.xs_1, s32[512,1]{1,0:T(8,128)} %get-tuple-element.69.clip, s32[512,1]{1,0:T(8,128)} %get-tuple-element.67.idc, s32[1,512]{1,0:T(1,128)} %copy-done.5, ...), custom_call_target="tpu_custom_call" | custom-call | flops 8000000000 | bytes 10000000 | tf_op jit(solution)/shard_map/pallas_call | solution.py:163
  147.8 1.4 pad_maximum_fusion.lse
  149.3 5.3 %shard_map.156 = (f32[512,768]{1,0:T(8,128)}, bf16[4,2,512,768]{3,2,1,0:T(8,128)(2,1)}) custom-call(s32[1]{0:T(128)} %bitcast.flag, f32[512,768]{1,0:T(8,128)} %get-tuple-element.37.x.xm_1, s32[512,1]{1,0:T(8,128)} %get-tuple-element.69.clip, f32[6,4,768]{2,1,0:T(4,128)} %get-tuple-element.70.mod, bf16[2,4,768,2304]{3,2,1,0:T(8,128)(2,1)} %get-tuple-element.34.w_hbm), custom_call_target="tpu_custom_call" | custom-call | flops 8000000000 | bytes 10000000 | tf_op jit(solution)/shard_map/pallas_call | solution.py:163
  154.5 2.4 convert_element_type.83.xb
  156.9 301.5 %shard_map.157 = (bf16[2,2,384,2304]{3,2,1,0:T(8,128)(2,1)}, bf16[2,384,2304]{2,1,0:T(8,128)(2,1)}, bf16[256,768]{1,0:T(8,128)(2,1)}, bf16[256,768]{1,0:T(8,128)(2,1)}) custom-call(bf16[512,768]{1,0:T(8,128)(2,1)} %convert_element_type.83.xb, bf16[1024,512]{1,0:T(8,128)(2,1)} %fusion.6.pick_t, f32[512,768]{1,0:T(8,128)} %fusion.1.g_in, ...), custom_call_target="tpu_custom_call" | custom-call | tf_op jit(solution)/shard_map/pallas_call | solution.py:977
  458.4 1.8 select_bitcast_fusion.1
  460.3 2.0 select_bitcast_fusion
  462.3 2.0 copy-done
  464.3 25.2 %shard_map.158 = (f32[2,384,2304]{2,1,0:T(8,128)}, f32[2,384,2304]{2,1,0:T(8,128)}, f32[2,384,2304]{2,1,0:T(8,128)}, f32[2,384,2304]{2,1,0:T(8,128)}, f32[2,384,...) custom-call(f32[2,384,2304]{2,1,0:T(8,128)} %par.3, f32[2,384,2304]{2,1,0:T(8,128)} %bitcast.37, f32[2,384,2304]{2,1,0:T(8,128)} %bitcast.39, ...), custom_call_target="tpu_custom_call" | custom-call | tf_op jit(solution)/shard_map/pallas_call | solution.py:1030
  (31 shorter events, 4.8 us)
Async XLA Ops:
  110.4 11.9 %copy-start.2 = (f32[4,9216]{1,0:T(4,128)}, f32[4,9216]{1,0:T(4,128)S(1)}, u32[]{:S(2)}) copy-start(f32[4,9216]{1,0:T(4,128)S(1)} %slice.19) | copy-start | bytes 442372
  113.2 3.8 copy-start.6
  121.0 9.9 %copy-start.5 = (s32[1,512]{1,0:T(1,128)}, s32[1,512]{1,0:T(1,128)S(1)}, u32[]{:S(2)}) copy-start(s32[1,512]{1,0:T(1,128)S(1)} %get-tuple-element.62.idr) | copy-start | bytes 6148
  121.6 9.2 %copy-start.4 = (s32[1,512]{1,0:T(1,128)}, s32[1,512]{1,0:T(1,128)S(1)}, u32[]{:S(2)}) copy-start(s32[1,512]{1,0:T(1,128)S(1)} %fusion.15.idr) | copy-start | bytes 6148
  141.6 6.3 %copy-start.3 = (f32[12,1,512]{2,1,0:T(1,128)S(1)}, f32[12,1,512]{2,1,0:T(1,128)}, u32[]{:S(2)}) copy-start(f32[12,1,512]{2,1,0:T(1,128)} %get-tuple-element.40) | copy-start | bytes 73732
  156.9 301.5 %copy-start.1 = (bf16[1,256,768]{2,1,0:T(8,128)(2,1)S(1)}, bf16[1,256,768]{2,1,0:T(8,128)(2,1)}, u32[]{:S(2)}) copy-start(bf16[1,256,768]{2,1,0:T(8,128)(2,1)} %param.9) | copy-start | bytes 1179652
  462.3 2.0 copy-start
